TPU v7x, 256 devices: a whole 4x4x8 slice. The times are simulated.
256 devices in a mesh: row: 8 (over x, core), col: 8 (over z_lo, y), rep: 4 (over z_hi).
Axes of the slice: x: 4, y: 4, z: 8 (z_hi: 4, z_lo: 2; z = z_hi * 2 + z_lo), core: 2. Of those that a mesh axis runs over, the one named last changes fastest.
Arguments:
- left_panel: float32 [1024, 16384], P(('col', 'rep'), 'row'), may hold values from -0.1875 to 0.1875
- right_panel: float32 [8, 4, 32, 16384], P(None, 'rep', 'row', 'col'), may hold values from -6 to 6
- left_mask: int32 [8, 128], replicated, may hold values from 0 to 1, as said below
- right_mask: int32 [8, 128], replicated, may hold values from 0 to 1, as said below
- accum: float32 [16384, 16384], P('row', ('col', 'rep')), may hold values from -6 to 6
Outputs:
- cube_acc: float32 [16384, 16384], P('row', ('col', 'rep'))
Inputs may be any that keep to these rules, and one draw needn't show every extreme that they name: `left_mask`: 1 marks an occupied tile, 0 an empty one. `right_mask`: 1 marks an occupied tile, 0 an empty one.
All inputs are finite; a program needn't handle non-finite values.
Results may differ from a plain program's by a relative error of at most 0.00005.
Values sent between devices are 32-bit elements; how exact they have to be, the bound alone decides.
No kernel may reach another device: no remote copies, remote signals or barrier semaphores. Data moves between devices by JAX's collectives and lax.ppermute only.
A program may use at most 64 MiB of HBM per device.

v0:
```python
import jax
import jax.numpy as jnp
from jax import lax
from jax.sharding import PartitionSpec as P


def mask_left(left_panel, left_mask):
    stretch, rows_dev = left_panel.shape
    n_rep = lax.axis_size("rep")
    row_tiles = rows_dev // 128
    k_start = (lax.axis_index("col") * n_rep + lax.axis_index("rep")) * stretch
    strip = lax.dynamic_slice(
        left_mask, (k_start // 128, lax.axis_index("row") * row_tiles), (1, row_tiles)
    ).astype(jnp.float32)
    shaped = left_panel.reshape(stretch, row_tiles, 128) * strip.reshape(1, row_tiles, 1)
    return shaped.reshape(stretch, rows_dev)


def mask_right(right_panel, right_mask):
    groups, single, piece, cols_dev = right_panel.shape
    n_rep = lax.axis_size("rep")
    span = piece * lax.axis_size("row")
    base = lax.axis_index("rep") * span + lax.axis_index("row") * piece
    starts = jnp.arange(groups, dtype=jnp.int32) * (n_rep * span) + base
    tile_ids = starts // 128
    onehot = (
        tile_ids[:, None] == jnp.arange(right_mask.shape[0], dtype=jnp.int32)[None, :]
    ).astype(jnp.float32)
    table = jnp.dot(
        onehot,
        right_mask.astype(jnp.float32),
        precision=lax.Precision.HIGHEST,
        preferred_element_type=jnp.float32,
    )
    col_tiles = cols_dev // 128
    chosen = lax.dynamic_slice_in_dim(table, lax.axis_index("col") * col_tiles, col_tiles, 1)
    shaped = right_panel.reshape(groups, single, piece, col_tiles, 128) * chosen.reshape(
        groups, 1, 1, col_tiles, 1
    )
    return shaped.reshape(groups, single, piece, cols_dev)


def contract(piece, right_rows):
    return lax.dot_general(
        piece,
        right_rows,
        (((0,), (0,)), ((), ())),
        precision=lax.Precision.HIGHEST,
        preferred_element_type=jnp.float32,
    )


def body(left_panel, right_panel, left_mask, right_mask, accum):
    left_local = mask_left(left_panel, left_mask)
    right_local = mask_right(right_panel, right_mask)
    parts = lax.all_to_all(right_local, "rep", split_axis=3, concat_axis=1, tiled=True)
    whole = lax.all_gather(parts, "row", axis=2, tiled=True)
    right_rows = whole.reshape(-1, whole.shape[3])
    total = contract(lax.all_gather(left_local, ("col", "rep"), axis=0, tiled=True), right_rows)
    return accum + total


def solution(mesh):
    return jax.shard_map(
        body,
        mesh=mesh,
        in_specs=(
            P(("col", "rep"), "row"),
            P(None, "rep", "row", "col"),
            P(),
            P(),
            P("row", ("col", "rep")),
        ),
        out_specs=P("row", ("col", "rep")),
        check_vma=False,
    )
```

profile of v0, /device:TPU:38, one launch (start us, length us, event | category | flops | bytes accessed | tf_op | source)
XLA Modules:
  0.0 316.9 jit_solution(18362587681494531938)
XLA Ops:
  6.5 0.0 all-gather.6.cloned.1.call-start
  6.5 0.9 fusion
  7.4 0.1 constant_dynamic-slice_fusion
  7.5 0.1 copy.13
  7.6 0.1 mul.67
  7.7 0.3 copy.18
  7.9 1.0 broadcast_multiply_fusion
  9.0 3.0 copy.15
  12.0 6.5 %reshape.41 = f32[4,1,16384]{2,1,0:T(1,128)S(1)} reshape(f32[2048,1,4,8]{3,2,1,0:T(4,128)} %bitcast.12) | data formatting | bytes 524288
  18.5 18.4 %all_to_all.18 = f32[4,1,16384]{2,1,0:T(1,128)S(1)} all-to-all(f32[4,1,16384]{2,1,0:T(1,128)S(1)} %reshape.41), channel_id=1, replica_groups=mesh['row'=8,'col'=8,'rep'=4] {'rep'}, dimensions={0} | all-to-all | bytes 524288 | tf_op jit(solution)/shard_map/all_to_all | solution.py:56
  36.9 0.5 broadcast.60
  37.4 1.4 reduce
  38.8 0.0 copy-start
  38.8 7.0 %reshape.42 = f32[2048,1,4,8]{3,2,1,0:T(4,128)} reshape(f32[4,16384]{1,0:T(4,128)S(1)} %reduce) | data formatting | bytes 524288
  45.8 4.4 %copy.16 = f32[8,1,4,4,512]{4,0,1,3,2:T(8,128)} copy(f32[8,1,4,4,512]{0,2,4,3,1:T(4,128)} %bitcast.13) | data formatting | bytes 524288 | tf_op jit(solution)/shard_map/all_to_all | solution.py:56
  50.2 0.0 all-gather.6.cloned.1.call-update
  50.3 0.2 all-gather.4.cloned.1.call-start
  50.5 0.8 convert_bitcast_fusion
  51.3 0.1 broadcast_bitcast_fusion
  51.4 0.0 copy-done
  51.4 0.7 broadcast_multiply_fusion.1
  52.1 0.0 all-gather.4.cloned.1.call-update
  52.1 22.7 %all-gather.6.cloned.1.call-done = f32[8,4,1,32,512]{4,0,2,1,3:T(8,128)} async-done(((f32[8,4,1,4,512]{4,0,2,1,3:T(8,128)}), f32[8,4,1,32,512]{4,0,2,1,3:T(8,128)}) %all-gather.6.cloned.1.call-update) | async-done | bytes 2097168 | tf_op jit(solution)/shard_map/all_gather | solution.py:57
  74.8 2.8 copy.17
  77.6 215.6 %all-gather.4.cloned.1.call-done = f32[1024,2048]{1,0:T(8,128)} async-done(((f32[32,2048]{1,0:T(8,128)}), f32[1024,2048]{1,0:T(8,128)}) %all-gather.4.cloned.1.call-update) | async-done | bytes 8388624 | tf_op jit(solution)/shard_map/all_gather | solution.py:59
  293.2 16.9 %convolution_add_fusion = f32[2048,512]{1,0:T(8,128)} fusion(f32[2048,512]{1,0:T(8,128)} %param.9, f32[1024,2048]{1,0:T(8,128)} %all-gather.4.cloned.1.call-done, f32[1024,512]{1,0:T(8,128)S(1)} %bitcast.14), kind=kOutput, calls=%fused_computation | convolution fusion | flops 12885950464 | bytes 18874368 | tf_op jit(solution)/shard_map/dot_general | solution.py:44
  (1 shorter events, 0.0 us)
Async XLA Ops:
  6.5 68.3 %all-gather.6.cloned.1.call-start = ((), (), s32[]{:S(2)}) async-start(), calls=%async_computation.2 | async-start | bytes 2359296 | tf_op jit(solution)/shard_map/all_gather | solution.py:57
  38.8 12.6 %copy-start = (f32[32,2048]{1,0:T(8,128)S(1)}, f32[32,2048]{1,0:T(8,128)}, u32[]{:S(2)}) copy-start(f32[32,2048]{1,0:T(8,128)} %param.5) | copy-start | bytes 786436
  50.3 242.9 %all-gather.4.cloned.1.call-start = ((), (), s32[]{:S(2)}) async-start(), calls=%async_computation.1 | async-start | bytes 8650752 | tf_op jit(solution)/shard_map/all_gather | solution.py:59
Sparse Core Ops, SparseCore 0:
  50.4 24.4 all-gather.5
  76.6 216.5 all-gather.3
where the time goes:
time: 317 us
  waiting for transfers between devices  238 us (75%)
  local copies, waits for them, and re-layouts  24.9 us (8%)
  blocking collectives  18.4 us (6%)
  matrix products  17.7 us (6%)
  between operations  13.5 us (4%)
  other arithmetic  3.91 us (1%)
    all_gather x1, waiting for transfers between devices, body(): lax.all_gather(left_local, ('col', 'rep'), axis=0, tiled=True)  216 us
    all_gather x1, waiting for transfers between devices, body(): whole = lax.all_gather(parts, 'row', axis=2, tiled=True)  22.7 us
    all_to_all x1, blocking collectives, body(): lax.all_to_all(right_local, 'rep', split_axis=3, concat_axis=1, tiled=True)  18.4 us
    dot_general x1, matrix products, contract(): lax.dot_general(piece, right_rows, (((0,), (0,)), ((), ())), precision=la...  16.9 us
    unnamed x5, local copies, waits for them, and re-layouts  13.8 us
  transfers between devices with their start and end apart: 2, of which 2 were waited for; matrix products, arithmetic and copies ran while one was open for 1% of the time, Pallas kernels for 0%

commit v1 on v0

v1 whole, which is shorter than its diff:
```python
import functools

import jax
import jax.numpy as jnp
from jax import lax
from jax.experimental import pallas as pl
from jax.experimental.pallas import tpu as pltpu
from jax.sharding import Mesh, PartitionSpec as P

KT = 128
Z = ("zlo", "zhi")
CA = 768
TN = 256


def z_slot(z):
    return (z % 2) * 4 + z // 2


def ring(n, step, slot=lambda i: i):
    return [(slot(i), slot((i + step) % n)) for i in range(n)]


def along_y(a, step):
    return lax.ppermute(a, "y", ring(4, step))


def along_z(a, step):
    return lax.ppermute(a, Z, ring(8, step, z_slot))


def along_x(a, step):
    return lax.ppermute(a, "x", ring(4, step))


def gather_y(own):
    half = own.shape[0] // 2
    up, down = along_y(own, 1), along_y(own, -1)
    return [own, up, down, along_y(up[:half], 1), along_y(down[half:], -1)]


def gather_z(own):
    half = own.shape[0] // 2
    up, down = [own], [own]
    for _ in range(3):
        up.append(along_z(up[-1], 1))
        down.append(along_z(down[-1], -1))
    last = [along_z(up[-1][:half], 1), along_z(down[-1][half:], -1)]
    return [own] + up[1:] + down[1:] + last


def right_kernel(place, own, up, down, far_a, far_b, mask, hi, lo, rows):
    x, rep = place[0], place[1]
    whole, front, back = range(4), range(2), range(2, 4)
    for dx, ref, sent in ((0, own, whole), (-1, up, whole), (1, down, whole), (2, far_a, front), (2, far_b, back)):
        for slot, s in enumerate(sent):
            base = lax.rem(rep - s + 4, 4) * 32 + lax.rem(x + dx + 4, 4) * 8
            for g in range(8):
                rows[pl.ds(pl.multiple_of(g * 128 + base, 8), 8), :] = ref[slot, g]
    for g in range(8):
        at = pl.ds(g * 128, 128)
        a = rows[at, :] * mask[pl.ds(g, 1), :]
        h = a.astype(jnp.bfloat16)
        hi[at, :] = h
        lo[at, :] = (a - h.astype(jnp.float32)).astype(jnp.bfloat16)


def assemble_right(place, pieces, mask):
    vm = pl.BlockSpec(memory_space=pltpu.VMEM)
    return pl.pallas_call(
        right_kernel,
        out_shape=[jax.ShapeDtypeStruct((1024, 512), jnp.bfloat16)] * 2,
        in_specs=[pl.BlockSpec(memory_space=pltpu.SMEM)] + [vm] * 6,
        out_specs=[vm, vm],
        scratch_shapes=[pltpu.VMEM((1024, 512), jnp.float32)],
        compiler_params=pltpu.CompilerParams(vmem_limit_bytes=24 * 2**20),
    )(place, *pieces, mask)


def product_kernel(heights, blocks, *refs):
    n = len(heights)
    pieces = refs[:n]
    mask, hi, lo, accum = refs[n : n + 4]
    out, lhi, llo = refs[-3:]
    j = 0
    for ref, height in zip(pieces, heights):
        for r in range(0, height, 32):
            kb = blocks[j]
            j += 1
            a = ref[r : r + 32, :] * mask[pl.ds(kb // 4, 1), :]
            h = a.astype(jnp.bfloat16)
            at = pl.ds(pl.multiple_of(kb * 32, 32), 32)
            lhi[at, :] = h
            llo[at, :] = (a - h.astype(jnp.float32)).astype(jnp.bfloat16)
    dot = functools.partial(
        lax.dot_general, dimension_numbers=(((0,), (0,)), ((), ())), preferred_element_type=jnp.float32
    )
    total = dot(lhi[...], lo[...]) + dot(llo[...], hi[...])
    out[...] = accum[...] + (total + dot(lhi[...], hi[...]))


def product(blocks, pieces, mask, hi, lo, accum, first, prev=None):
    heights = tuple(p.shape[0] for p in pieces)
    width = pieces[0].shape[1]
    skip = first // TN
    n = len(pieces)

    def wrapped(blocks_ref, *refs):
        refs = list(refs)
        if prev is not None:
            del refs[n + 4]
        product_kernel(heights, blocks_ref, *refs)

    in_specs = [pl.BlockSpec((h, TN), lambda i, b: (0, i)) for h in heights]
    in_specs += [
        pl.BlockSpec((8, TN), lambda i, b: (0, i + skip)),
        pl.BlockSpec((1024, 512), lambda i, b: (0, 0)),
        pl.BlockSpec((1024, 512), lambda i, b: (0, 0)),
        pl.BlockSpec((TN, 512), lambda i, b: (i + skip, 0)),
    ]
    args = [blocks, *pieces, mask, hi, lo, accum]
    aliases = {}
    if prev is not None:
        in_specs.append(pl.BlockSpec(memory_space=pl.ANY))
        aliases = {len(args): 0}
        args.append(prev)
    return pl.pallas_call(
        wrapped,
        out_shape=jax.ShapeDtypeStruct(accum.shape, jnp.float32),
        grid_spec=pltpu.PrefetchScalarGridSpec(
            num_scalar_prefetch=1,
            grid=(width // TN,),
            in_specs=in_specs,
            out_specs=pl.BlockSpec((TN, 512), lambda i, b: (i + skip, 0)),
            scratch_shapes=[pltpu.VMEM((1024, TN), jnp.bfloat16)] * 2,
        ),
        input_output_aliases=aliases,
        compiler_params=pltpu.CompilerParams(vmem_limit_bytes=24 * 2**20),
        cost_estimate=pl.CostEstimate(
            flops=2 * 3 * 1024 * width * 512,
            bytes_accessed=1024 * width * 4 + width * 512 * 8 + 2**21,
            transcendentals=0,
        ),
    )(*args)


def body(left, right, left_mask, right_mask, accum):
    x, core, y = (lax.axis_index(a) for a in ("x", "core", "y"))
    zlo, rep = lax.axis_index("zlo"), lax.axis_index("zhi")
    z = rep * 2 + zlo
    row, col = x * 2 + core, zlo * 4 + y

    a_own = jnp.concatenate(gather_y(left[:, :CA]), 0)
    a = gather_z(a_own)
    b_own = jnp.concatenate(gather_z(left[:, CA:]), 0)
    b = gather_y(b_own)

    def block(dy, dz):
        yy, zz = (y + dy) % 4, (z + dz) % 8
        return ((zz % 2) * 4 + yy) * 4 + zz // 2

    z_order = (0, -1, -2, -3, 1, 2, 3, 4)
    y_order = (0, -1, 1, 2)
    a_blocks = jnp.stack([block(dy, dz) for dz in z_order for dy in y_order]).astype(jnp.int32)
    b_blocks = jnp.stack([block(dy, dz) for dy in y_order for dz in z_order]).astype(jnp.int32)

    layers = []
    for s in range(4):
        owner = (rep + s) % 4
        part = lax.dynamic_slice_in_dim(right, owner * 512, 512, 3)[:, 0]
        layers.append(part if s == 0 else lax.ppermute(part, "zhi", ring(4, s)))
    layers = jnp.stack(layers)
    other = lax.ppermute(layers, "core", [(0, 1), (1, 0)])
    first, second = jnp.where(core == 0, layers, other), jnp.where(core == 0, other, layers)
    both = jnp.concatenate([first, second], 2)
    up, down = along_x(both, 1), along_x(both, -1)
    far_a, far_b = along_x(up[:2], 1), along_x(down[2:], -1)
    right_tiles = lax.dynamic_slice(right_mask, (0, col * 16 + rep * 4), (8, 4)).astype(jnp.float32)
    place = jnp.stack([x, rep]).astype(jnp.int32)
    hi, lo = assemble_right(place, [both, up, down, far_a, far_b], jnp.repeat(right_tiles, KT, axis=1))

    left_tiles = lax.dynamic_slice(left_mask, (0, row * 16), (8, 16)).astype(jnp.float32)
    mask = jnp.repeat(left_tiles, KT, axis=1)
    out = product(a_blocks, a, mask, hi, lo, accum, 0)
    return product(b_blocks, b, mask, hi, lo, accum, CA, out)


def solution(mesh):
    fine = Mesh(mesh.devices.reshape(4, 2, 2, 4, 4), ("x", "core", "zlo", "y", "zhi"))
    row, col, rep = ("x", "core"), ("zlo", "y"), ("zhi",)
    return jax.shard_map(
        body,
        mesh=fine,
        in_specs=(P(col + rep, row), P(None, rep, row, col), P(), P(), P(row, col + rep)),
        out_specs=P(row, col + rep),
        check_vma=False,
    )
```

time: 317 us -> 117 us (0.37)
  the two profiles are of different devices: /device:TPU:38 before, /device:TPU:2 now
where the time goes in v1:
time: 117 us
  starting transfers between devices  45.6 us (39%)
  waiting for transfers between devices  33 us (28%)
  local copies, waits for them, and re-layouts  19.5 us (17%)
  Pallas kernels  18.1 us (15%)
    ppermute x16, waiting for transfers between devices, along_z(): return lax.ppermute(a, Z, ring(8, step, z_slot))  23.7 us
    ppermute x16, starting transfers between devices, along_z(): return lax.ppermute(a, Z, ring(8, step, z_slot))  19.2 us
    pallas_call x2, Pallas kernels, product(): pl.pallas_call(wrapped, out_shape=jax.ShapeDtypeStruct(accum.shape, jnp.f...  16.1 us
    ppermute x3, starting transfers between devices, body(): layers.append(part if s == 0 else lax.ppermute(part, 'zhi', ring(4, s)))  11.4 us
    ppermute x8, starting transfers between devices, along_y(): return lax.ppermute(a, 'y', ring(4, step))  11.3 us
    ppermute x8, waiting for transfers between devices, along_y(): return lax.ppermute(a, 'y', ring(4, step))  8.66 us
    unnamed x28, local copies, waits for them, and re-layouts  6.94 us
    ppermute x4, starting transfers between devices, along_x(): return lax.ppermute(a, 'x', ring(4, step))  3.6 us
  transfers between devices with their start and end apart: 32, of which 11 were waited for; matrix products, arithmetic and copies ran while one was open for 14% of the time, Pallas kernels for 8%

profile of v1, /device:TPU:2, one launch (start us, length us, event | category | flops | bytes accessed | tf_op | source)
XLA Modules:
  0.0 117.1 jit_solution(902719122904138998)
XLA Ops:
  0.9 3.1 %collective-permute-start.21 = (f32[32,768]{1,0:T(8,128)S(1)}, f32[32,768]{1,0:T(8,128)S(1)}, u32[]{:S(2)}, u32[]{:S(2)}) collective-permute-start(f32[32,768]{1,0:T(8,128)S(1)} %get-tuple-element.11), channel_id=1, source_target_pairs={{0,12},{4,0},{8,4},{12,8},{1,13},{5,1},{9,5},{13,9},{2,14},{6,2},{... | collective-permute-start | bytes 294920 | tf_op jit(solution)/shard_map/ppermute | solution.py:25
  4.0 1.0 dynamic-slice_bitcast_fusion.3
  5.0 3.3 %collective-permute-start.12 = (f32[8,4,512]{2,1,0:T(4,128)S(1)}, f32[8,4,512]{2,1,0:T(4,128)S(1)}, u32[]{:S(2)}, u32[]{:S(2)}) collective-permute-start(f32[8,4,512]{2,1,0:T(4,128)S(1)} %get-tuple-element.14), channel_id=1, source_target_pairs={{0,1},{1,2},{2,3},{3,0},{4,5},{5,6},{6,7},{7,4},{8,9},{9,10},{10,1... | collective-permute-start | bytes 196616 | tf_op jit(solution)/shard_map/ppermute | solution.py:171
  8.3 3.1 %collective-permute-start.14 = (f32[8,4,512]{2,1,0:T(4,128)S(1)}, f32[8,4,512]{2,1,0:T(4,128)S(1)}, u32[]{:S(2)}, u32[]{:S(2)}) collective-permute-start(f32[8,4,512]{2,1,0:T(4,128)S(1)} %get-tuple-element.15), channel_id=1, source_target_pairs={{0,3},{1,0},{2,1},{3,2},{4,7},{5,4},{6,5},{7,6},{8,11},{9,8},{10,9... | collective-permute-start | bytes 196616 | tf_op jit(solution)/shard_map/ppermute | solution.py:171
  11.4 4.9 %collective-permute-start.13 = (f32[8,4,512]{2,1,0:T(4,128)S(1)}, f32[8,4,512]{2,1,0:T(4,128)S(1)}, u32[]{:S(2)}, u32[]{:S(2)}) collective-permute-start(f32[8,4,512]{2,1,0:T(4,128)S(1)} %get-tuple-element.16), channel_id=1, source_target_pairs={{0,2},{1,3},{2,0},{3,1},{4,6},{5,7},{6,4},{7,5},{8,10},{9,11},{10,... | collective-permute-start | bytes 196616 | tf_op jit(solution)/shard_map/ppermute | solution.py:171
  16.4 1.6 %fusion.1 = (f32[32,1280]{1,0:T(8,128)S(1)}, f32[256,1280]{1,0:T(8,128)}) fusion(f32[32,2048]{1,0:T(8,128)} %param.5), kind=kLoop, calls=%fused_computation.28 | loop fusion | bytes 491520 | tf_op jit(solution)/shard_map/slice | solution.py:155
  18.0 2.0 %collective-permute-start = (f32[32,1280]{1,0:T(8,128)S(1)}, f32[32,1280]{1,0:T(8,128)S(1)}, u32[]{:S(2)}, u32[]{:S(2)}) collective-permute-start(f32[32,1280]{1,0:T(8,128)S(1)} %get-tuple-element.17), channel_id=1, source_target_pairs={{0,16},{16,1},{1,17},{17,2},{2,18},{18,3},{3,19},{19,0},{4,20},{20... | collective-permute-start | bytes 491528 | tf_op jit(solution)/shard_map/ppermute | solution.py:29
  20.6 3.3 %collective-permute-start.23 = (f32[16,768]{1,0:T(8,128)S(1)}, f32[16,768]{1,0:T(8,128)S(1)}, u32[]{:S(2)}, u32[]{:S(2)}) collective-permute-start(f32[16,768]{1,0:T(8,128)S(1)} %slice.55), channel_id=1, source_target_pairs={{0,12},{4,0},{8,4},{12,8},{1,13},{5,1},{9,5},{13,9},{2,14},{6,2},{... | collective-permute-start | bytes 147464 | tf_op jit(solution)/shard_map/ppermute | solution.py:25
  24.1 2.8 %collective-permute-start.4 = (f32[32,1280]{1,0:T(8,128)S(1)}, f32[32,1280]{1,0:T(8,128)S(1)}, u32[]{:S(2)}, u32[]{:S(2)}) collective-permute-start(f32[32,1280]{1,0:T(8,128)S(1)} %collective-permute-done.3), channel_id=1, source_target_pairs={{0,19},{16,0},{1,16},{17,1},{2,17},{18,2},{3,18},{19,3},{4,23},{20... | collective-permute-start | bytes 491528 | tf_op jit(solution)/shard_map/ppermute | solution.py:29
  27.5 3.7 %collective-permute-done.4 = f32[32,1280]{1,0:T(8,128)S(1)} collective-permute-done((f32[32,1280]{1,0:T(8,128)S(1)}, f32[32,1280]{1,0:T(8,128)S(1)}, u32[]{:S(2)}, u32[]{:S(2)}) %collective-permute-start.4) | collective-permute-done | bytes 163872 | tf_op jit(solution)/shard_map/ppermute | solution.py:29
  31.3 3.1 %collective-permute-start.5 = (f32[32,1280]{1,0:T(8,128)S(1)}, f32[32,1280]{1,0:T(8,128)S(1)}, u32[]{:S(2)}, u32[]{:S(2)}) collective-permute-start(f32[32,1280]{1,0:T(8,128)S(1)} %collective-permute-done.4), channel_id=1, source_target_pairs={{0,19},{16,0},{1,16},{17,1},{2,17},{18,2},{3,18},{19,3},{4,23},{20... | collective-permute-start | bytes 491528 | tf_op jit(solution)/shard_map/ppermute | solution.py:29
  35.0 2.3 %collective-permute-done.5 = f32[32,1280]{1,0:T(8,128)S(1)} collective-permute-done((f32[32,1280]{1,0:T(8,128)S(1)}, f32[32,1280]{1,0:T(8,128)S(1)}, u32[]{:S(2)}, u32[]{:S(2)}) %collective-permute-start.5) | collective-permute-done | bytes 163872 | tf_op jit(solution)/shard_map/ppermute | solution.py:29
  37.3 3.7 %collective-permute-start.7 = (f32[16,1280]{1,0:T(8,128)S(1)}, f32[16,1280]{1,0:T(8,128)S(1)}, u32[]{:S(2)}, u32[]{:S(2)}) collective-permute-start(f32[16,1280]{1,0:T(8,128)S(1)} %slice.49), channel_id=1, source_target_pairs={{0,19},{16,0},{1,16},{17,1},{2,17},{18,2},{3,18},{19,3},{4,23},{20... | collective-permute-start | bytes 245768 | tf_op jit(solution)/shard_map/ppermute | solution.py:29
  44.0 2.9 %collective-permute-done.6 = f32[16,1280]{1,0:T(8,128)S(1)} collective-permute-done((f32[16,1280]{1,0:T(8,128)S(1)}, f32[16,1280]{1,0:T(8,128)S(1)}, u32[]{:S(2)}, u32[]{:S(2)}) %collective-permute-start.6) | collective-permute-done | bytes 81952 | tf_op jit(solution)/shard_map/ppermute | solution.py:29
  48.2 2.8 %collective-permute-start.9 = (f32[256,1280]{1,0:T(8,128)}, f32[256,1280]{1,0:T(8,128)S(1)}, u32[]{:S(2)}, u32[]{:S(2)}) collective-permute-start(f32[256,1280]{1,0:T(8,128)} %constant_dynamic-update-slice_fusion.refs_0_), channel_id=1, source_target_pairs={{0,12},{4,0},{8,4},{12,8},{1,13},{5,1},{9,5},{13,9},{2,14},{6,2},{... | collective-permute-start | bytes 3932168 | tf_op jit(solution)/shard_map/ppermute | solution.py:25
  51.5 1.7 %collective-permute-start.24 = (f32[128,768]{1,0:T(8,128)S(1)}, f32[128,768]{1,0:T(8,128)}, u32[]{:S(2)}, u32[]{:S(2)}) collective-permute-start(f32[128,768]{1,0:T(8,128)S(1)} %constant_dynamic-update-slice_fusion.9.refs_0_), channel_id=1, source_target_pairs={{0,16},{16,1},{1,17},{17,2},{2,18},{18,3},{3,19},{19,0},{4,20},{20... | collective-permute-start | bytes 1179656 | tf_op jit(solution)/shard_map/ppermute | solution.py:29
  54.1 6.8 %collective-permute-done.27.refs_4_ = f32[128,768]{1,0:T(8,128)} collective-permute-done((f32[128,768]{1,0:T(8,128)S(1)}, f32[128,768]{1,0:T(8,128)}, u32[]{:S(2)}, u32[]{:S(2)}) %collective-permute-start.27) | collective-permute-done | bytes 393248 | tf_op jit(solution)/shard_map/ppermute | solution.py:29
  60.9 2.0 %collective-permute-start.25 = (f32[128,768]{1,0:T(8,128)}, f32[128,768]{1,0:T(8,128)}, u32[]{:S(2)}, u32[]{:S(2)}) collective-permute-start(f32[128,768]{1,0:T(8,128)} %collective-permute-done.24.refs_1_), channel_id=1, source_target_pairs={{0,16},{16,1},{1,17},{17,2},{2,18},{18,3},{3,19},{19,0},{4,20},{20... | collective-permute-start | bytes 1179656 | tf_op jit(solution)/shard_map/ppermute | solution.py:29
  63.1 1.5 %collective-permute-start.16 = (f32[4,8,8,512]{3,2,1,0:T(8,128)S(1)}, f32[4,8,8,512]{3,2,1,0:T(8,128)}, u32[]{:S(2)}, u32[]{:S(2)}) collective-permute-start(f32[4,8,8,512]{3,2,1,0:T(8,128)S(1)} %pad_maximum_fusion.own), channel_id=1, source_target_pairs={{0,64},{64,128},{128,192},{192,0},{1,65},{65,129},{129,193},{193,1... | collective-permute-start | bytes 1572872 | tf_op jit(solution)/shard_map/ppermute | solution.py:33
  64.7 1.7 %slice.53 = f32[2,8,8,512]{3,2,1,0:T(8,128)} slice(f32[4,8,8,512]{3,2,1,0:T(8,128)} %collective-permute-done.17.down), slice={[2:4], [0:8], [0:8], [0:512]} | slice | bytes 524288 | tf_op jit(solution)/shard_map/slice | solution.py:177
  66.4 3.4 %collective-permute-done.28.refs_5_ = f32[128,768]{1,0:T(8,128)} collective-permute-done((f32[128,768]{1,0:T(8,128)}, f32[128,768]{1,0:T(8,128)}, u32[]{:S(2)}, u32[]{:S(2)}) %collective-permute-start.28) | collective-permute-done | bytes 393248 | tf_op jit(solution)/shard_map/ppermute | solution.py:29
  70.7 5.5 %collective-permute-done.9.refs_2_ = f32[256,1280]{1,0:T(8,128)S(1)} collective-permute-done((f32[256,1280]{1,0:T(8,128)}, f32[256,1280]{1,0:T(8,128)S(1)}, u32[]{:S(2)}, u32[]{:S(2)}) %collective-permute-start.9) | collective-permute-done | bytes 1310752 | tf_op jit(solution)/shard_map/ppermute | solution.py:25
  77.7 3.2 %collective-permute-done.8.refs_1_ = f32[256,1280]{1,0:T(8,128)S(1)} collective-permute-done((f32[256,1280]{1,0:T(8,128)}, f32[256,1280]{1,0:T(8,128)S(1)}, u32[]{:S(2)}, u32[]{:S(2)}) %collective-permute-start.8) | collective-permute-done | bytes 1310752 | tf_op jit(solution)/shard_map/ppermute | solution.py:25
  82.1 1.8 %collective-permute-start.10 = (f32[128,1280]{1,0:T(8,128)}, f32[128,1280]{1,0:T(8,128)}, u32[]{:S(2)}, u32[]{:S(2)}) collective-permute-start(f32[128,1280]{1,0:T(8,128)} %slice.50), channel_id=1, source_target_pairs={{0,4},{4,8},{8,12},{12,0},{1,5},{5,9},{9,13},{13,1},{2,6},{6,10},{... | collective-permute-start | bytes 1966088 | tf_op jit(solution)/shard_map/ppermute | solution.py:25
  83.9 1.7 %slice.52 = f32[2,8,8,512]{3,2,1,0:T(8,128)} slice(f32[4,8,8,512]{3,2,1,0:T(8,128)} %collective-permute-done.16.up), slice={[0:2], [0:8], [0:8], [0:512]} | slice | bytes 524288 | tf_op jit(solution)/shard_map/slice | solution.py:177
  85.6 1.5 %collective-permute-start.18 = (f32[2,8,8,512]{3,2,1,0:T(8,128)}, f32[2,8,8,512]{3,2,1,0:T(8,128)}, u32[]{:S(2)}, u32[]{:S(2)}) collective-permute-start(f32[2,8,8,512]{3,2,1,0:T(8,128)} %slice.52), channel_id=1, source_target_pairs={{0,64},{64,128},{128,192},{192,0},{1,65},{65,129},{129,193},{193,1... | collective-permute-start | bytes 786440 | tf_op jit(solution)/shard_map/ppermute | solution.py:33
  88.1 2.7 %collective-permute-start.31 = (f32[64,768]{1,0:T(8,128)S(1)}, f32[64,768]{1,0:T(8,128)S(1)}, u32[]{:S(2)}, u32[]{:S(2)}) collective-permute-start(f32[64,768]{1,0:T(8,128)S(1)} %slice.57), channel_id=1, source_target_pairs={{0,19},{16,0},{1,16},{17,1},{2,17},{18,2},{3,18},{19,3},{4,23},{20... | collective-permute-start | bytes 589832 | tf_op jit(solution)/shard_map/ppermute | solution.py:29
  92.6 2.0 %shard_map.55 = (bf16[1024,512]{1,0:T(8,128)(2,1)S(1)}, bf16[1024,512]{1,0:T(8,128)(2,1)S(1)}) custom-call(s32[2]{0:T(128)S(1)} %pad_add_fusion.place, f32[4,8,8,512]{3,2,1,0:T(8,128)S(1)} %pad_maximum_fusion.own, f32[4,8,8,512]{3,2,1,0:T(8,128)} %collective-permute-done.16.up, f32[4,8,8,512]{3,2,1,0:T(8,128)} %collective-permute-done.17.down, ...), custom_call_target="tpu_custom_call" | custom-call | tf_op jit(solution)/shard_map/pallas_call | solution.py:70
  94.6 4.1 %collective-permute-done.30.refs_7_ = f32[64,768]{1,0:T(8,128)S(1)} collective-permute-done((f32[64,768]{1,0:T(8,128)S(1)}, f32[64,768]{1,0:T(8,128)S(1)}, u32[]{:S(2)}, u32[]{:S(2)}) %collective-permute-start.30) | collective-permute-done | bytes 196640 | tf_op jit(solution)/shard_map/ppermute | solution.py:29
  98.7 2.2 %copy-done = f32[2048,512]{1,0:T(8,128)S(1)} copy-done((f32[2048,512]{1,0:T(8,128)S(1)}, f32[2048,512]{1,0:T(8,128)}, u32[]{:S(2)}) %copy-start) | copy-done | bytes 4194328
  100.9 6.9 %shard_map.56.refs_9_ = f32[2048,512]{1,0:T(8,128)} custom-call(s32[32]{0:T(128)S(1)} %stack.195.blocks_ref, f32[128,768]{1,0:T(8,128)S(1)} %copy-done.3, f32[128,768]{1,0:T(8,128)} %collective-permute-done.24.refs_1_, f32[128,768]{1,0:T(8,128)} %collective-permute-done.25.refs_2_, f32[128,768]{1,0:T(8,128)} %collective-permute-done.26.refs_3_, ...), custom_call_target="tpu_custom_call" | custom-call | flops 2415919104 | bytes 8388608 | tf_op jit(solution)/shard_map/pallas_call | solution.py:127
  107.8 9.3 %shard_map.57 = f32[2048,512]{1,0:T(8,128)} custom-call(s32[32]{0:T(128)S(1)} %stack.187.blocks_ref, f32[256,1280]{1,0:T(8,128)} %constant_dynamic-update-slice_fusion.refs_0_, f32[256,1280]{1,0:T(8,128)S(1)} %collective-permute-done.8.refs_1_, f32[256,1280]{1,0:T(8,128)S(1)} %collective-permute-done.9.refs_2_, ...), custom_call_target="tpu_custom_call", output_to_operand_aliasing={{}: (10, {})} | custom-call | flops 4026531840 | bytes 12582912 | tf_op jit(solution)/shard_map/pallas_call | solution.py:127
  (90 shorter events, 15.3 us)
Async XLA Ops:
  0.9 19.7 %collective-permute-start.21 = (f32[32,768]{1,0:T(8,128)S(1)}, f32[32,768]{1,0:T(8,128)S(1)}, u32[]{:S(2)}, u32[]{:S(2)}) collective-permute-start(f32[32,768]{1,0:T(8,128)S(1)} %get-tuple-element.11), channel_id=1, source_target_pairs={{0,12},{4,0},{8,4},{12,8},{1,13},{5,1},{9,5},{13,9},{2,14},{6,2},{... | collective-permute-start | bytes 294920 | tf_op jit(solution)/shard_map/ppermute | solution.py:25
  4.0 19.9 %collective-permute-start.20 = (f32[32,768]{1,0:T(8,128)S(1)}, f32[32,768]{1,0:T(8,128)S(1)}, u32[]{:S(2)}, u32[]{:S(2)}) collective-permute-start(f32[32,768]{1,0:T(8,128)S(1)} %get-tuple-element.11), channel_id=1, source_target_pairs={{0,4},{4,8},{8,12},{12,0},{1,5},{5,9},{9,13},{13,1},{2,6},{6,10},{... | collective-permute-start | bytes 294920 | tf_op jit(solution)/shard_map/ppermute | solution.py:25
  5.0 13.0 %collective-permute-start.12 = (f32[8,4,512]{2,1,0:T(4,128)S(1)}, f32[8,4,512]{2,1,0:T(4,128)S(1)}, u32[]{:S(2)}, u32[]{:S(2)}) collective-permute-start(f32[8,4,512]{2,1,0:T(4,128)S(1)} %get-tuple-element.14), channel_id=1, source_target_pairs={{0,1},{1,2},{2,3},{3,0},{4,5},{5,6},{6,7},{7,4},{8,9},{9,10},{10,1... | collective-permute-start | bytes 196616 | tf_op jit(solution)/shard_map/ppermute | solution.py:171
  8.3 9.7 %collective-permute-start.14 = (f32[8,4,512]{2,1,0:T(4,128)S(1)}, f32[8,4,512]{2,1,0:T(4,128)S(1)}, u32[]{:S(2)}, u32[]{:S(2)}) collective-permute-start(f32[8,4,512]{2,1,0:T(4,128)S(1)} %get-tuple-element.15), channel_id=1, source_target_pairs={{0,3},{1,0},{2,1},{3,2},{4,7},{5,4},{6,5},{7,6},{8,11},{9,8},{10,9... | collective-permute-start | bytes 196616 | tf_op jit(solution)/shard_map/ppermute | solution.py:171
  11.4 9.0 %collective-permute-start.13 = (f32[8,4,512]{2,1,0:T(4,128)S(1)}, f32[8,4,512]{2,1,0:T(4,128)S(1)}, u32[]{:S(2)}, u32[]{:S(2)}) collective-permute-start(f32[8,4,512]{2,1,0:T(4,128)S(1)} %get-tuple-element.16), channel_id=1, source_target_pairs={{0,2},{1,3},{2,0},{3,1},{4,6},{5,7},{6,4},{7,5},{8,10},{9,11},{10,... | collective-permute-start | bytes 196616 | tf_op jit(solution)/shard_map/ppermute | solution.py:171
  18.0 6.1 %collective-permute-start.3 = (f32[32,1280]{1,0:T(8,128)S(1)}, f32[32,1280]{1,0:T(8,128)S(1)}, u32[]{:S(2)}, u32[]{:S(2)}) collective-permute-start(f32[32,1280]{1,0:T(8,128)S(1)} %get-tuple-element.17), channel_id=1, source_target_pairs={{0,19},{16,0},{1,16},{17,1},{2,17},{18,2},{3,18},{19,3},{4,23},{20... | collective-permute-start | bytes 491528 | tf_op jit(solution)/shard_map/ppermute | solution.py:29
  18.0 8.9 %collective-permute-start = (f32[32,1280]{1,0:T(8,128)S(1)}, f32[32,1280]{1,0:T(8,128)S(1)}, u32[]{:S(2)}, u32[]{:S(2)}) collective-permute-start(f32[32,1280]{1,0:T(8,128)S(1)} %get-tuple-element.17), channel_id=1, source_target_pairs={{0,16},{16,1},{1,17},{17,2},{2,18},{18,3},{3,19},{19,0},{4,20},{20... | collective-permute-start | bytes 491528 | tf_op jit(solution)/shard_map/ppermute | solution.py:29
  20.5 32.7 %collective-permute-start.15 = (f32[4,8,4,512]{3,2,1,0:T(4,128)S(1)}, f32[4,8,4,512]{3,2,1,0:T(4,128)S(1)}, u32[]{:S(2)}, u32[]{:S(2)}) collective-permute-start(f32[4,8,4,512]{3,2,1,0:T(4,128)S(1)} %pad_maximum_fusion.1), channel_id=1, source_target_pairs={{0,32},{32,0},{1,33},{33,1},{2,34},{34,2},{3,35},{35,3},{4,36},{36... | collective-permute-start | bytes 786440 | tf_op jit(solution)/shard_map/ppermute | solution.py:173
  20.6 30.4 %collective-permute-start.23 = (f32[16,768]{1,0:T(8,128)S(1)}, f32[16,768]{1,0:T(8,128)S(1)}, u32[]{:S(2)}, u32[]{:S(2)}) collective-permute-start(f32[16,768]{1,0:T(8,128)S(1)} %slice.55), channel_id=1, source_target_pairs={{0,12},{4,0},{8,4},{12,8},{1,13},{5,1},{9,5},{13,9},{2,14},{6,2},{... | collective-permute-start | bytes 147464 | tf_op jit(solution)/shard_map/ppermute | solution.py:25
  24.0 27.1 %collective-permute-start.22 = (f32[16,768]{1,0:T(8,128)S(1)}, f32[16,768]{1,0:T(8,128)S(1)}, u32[]{:S(2)}, u32[]{:S(2)}) collective-permute-start(f32[16,768]{1,0:T(8,128)S(1)} %slice.54), channel_id=1, source_target_pairs={{0,4},{4,8},{8,12},{12,0},{1,5},{5,9},{9,13},{13,1},{2,6},{6,10},{... | collective-permute-start | bytes 147464 | tf_op jit(solution)/shard_map/ppermute | solution.py:25
  24.1 7.2 %collective-permute-start.4 = (f32[32,1280]{1,0:T(8,128)S(1)}, f32[32,1280]{1,0:T(8,128)S(1)}, u32[]{:S(2)}, u32[]{:S(2)}) collective-permute-start(f32[32,1280]{1,0:T(8,128)S(1)} %collective-permute-done.3), channel_id=1, source_target_pairs={{0,19},{16,0},{1,16},{17,1},{2,17},{18,2},{3,18},{19,3},{4,23},{20... | collective-permute-start | bytes 491528 | tf_op jit(solution)/shard_map/ppermute | solution.py:29
  26.8 7.5 %collective-permute-start.1 = (f32[32,1280]{1,0:T(8,128)S(1)}, f32[32,1280]{1,0:T(8,128)S(1)}, u32[]{:S(2)}, u32[]{:S(2)}) collective-permute-start(f32[32,1280]{1,0:T(8,128)S(1)} %collective-permute-done), channel_id=1, source_target_pairs={{0,16},{16,1},{1,17},{17,2},{2,18},{18,3},{3,19},{19,0},{4,20},{20... | collective-permute-start | bytes 491528 | tf_op jit(solution)/shard_map/ppermute | solution.py:29
  31.3 6.1 %collective-permute-start.5 = (f32[32,1280]{1,0:T(8,128)S(1)}, f32[32,1280]{1,0:T(8,128)S(1)}, u32[]{:S(2)}, u32[]{:S(2)}) collective-permute-start(f32[32,1280]{1,0:T(8,128)S(1)} %collective-permute-done.4), channel_id=1, source_target_pairs={{0,19},{16,0},{1,16},{17,1},{2,17},{18,2},{3,18},{19,3},{4,23},{20... | collective-permute-start | bytes 491528 | tf_op jit(solution)/shard_map/ppermute | solution.py:29
  34.3 6.7 %collective-permute-start.2 = (f32[32,1280]{1,0:T(8,128)S(1)}, f32[32,1280]{1,0:T(8,128)S(1)}, u32[]{:S(2)}, u32[]{:S(2)}) collective-permute-start(f32[32,1280]{1,0:T(8,128)S(1)} %collective-permute-done.1), channel_id=1, source_target_pairs={{0,16},{16,1},{1,17},{17,2},{2,18},{18,3},{3,19},{19,0},{4,20},{20... | collective-permute-start | bytes 491528 | tf_op jit(solution)/shard_map/ppermute | solution.py:29
  37.3 10.3 %collective-permute-start.7 = (f32[16,1280]{1,0:T(8,128)S(1)}, f32[16,1280]{1,0:T(8,128)S(1)}, u32[]{:S(2)}, u32[]{:S(2)}) collective-permute-start(f32[16,1280]{1,0:T(8,128)S(1)} %slice.49), channel_id=1, source_target_pairs={{0,19},{16,0},{1,16},{17,1},{2,17},{18,2},{3,18},{19,3},{4,23},{20... | collective-permute-start | bytes 245768 | tf_op jit(solution)/shard_map/ppermute | solution.py:29
  41.0 5.9 %collective-permute-start.6 = (f32[16,1280]{1,0:T(8,128)S(1)}, f32[16,1280]{1,0:T(8,128)S(1)}, u32[]{:S(2)}, u32[]{:S(2)}) collective-permute-start(f32[16,1280]{1,0:T(8,128)S(1)} %slice.48), channel_id=1, source_target_pairs={{0,16},{16,1},{1,17},{17,2},{2,18},{18,3},{3,19},{19,0},{4,20},{20... | collective-permute-start | bytes 245768 | tf_op jit(solution)/shard_map/ppermute | solution.py:29
  48.2 27.9 %collective-permute-start.9 = (f32[256,1280]{1,0:T(8,128)}, f32[256,1280]{1,0:T(8,128)S(1)}, u32[]{:S(2)}, u32[]{:S(2)}) collective-permute-start(f32[256,1280]{1,0:T(8,128)} %constant_dynamic-update-slice_fusion.refs_0_), channel_id=1, source_target_pairs={{0,12},{4,0},{8,4},{12,8},{1,13},{5,1},{9,5},{13,9},{2,14},{6,2},{... | collective-permute-start | bytes 3932168 | tf_op jit(solution)/shard_map/ppermute | solution.py:25
  51.1 9.7 %collective-permute-start.27 = (f32[128,768]{1,0:T(8,128)S(1)}, f32[128,768]{1,0:T(8,128)}, u32[]{:S(2)}, u32[]{:S(2)}) collective-permute-start(f32[128,768]{1,0:T(8,128)S(1)} %constant_dynamic-update-slice_fusion.9.refs_0_), channel_id=1, source_target_pairs={{0,19},{16,0},{1,16},{17,1},{2,17},{18,2},{3,18},{19,3},{4,23},{20... | collective-permute-start | bytes 1179656 | tf_op jit(solution)/shard_map/ppermute | solution.py:29
  51.5 9.4 %collective-permute-start.24 = (f32[128,768]{1,0:T(8,128)S(1)}, f32[128,768]{1,0:T(8,128)}, u32[]{:S(2)}, u32[]{:S(2)}) collective-permute-start(f32[128,768]{1,0:T(8,128)S(1)} %constant_dynamic-update-slice_fusion.9.refs_0_), channel_id=1, source_target_pairs={{0,16},{16,1},{1,17},{17,2},{2,18},{18,3},{3,19},{19,0},{4,20},{20... | collective-permute-start | bytes 1179656 | tf_op jit(solution)/shard_map/ppermute | solution.py:29
  53.2 27.7 %collective-permute-start.8 = (f32[256,1280]{1,0:T(8,128)}, f32[256,1280]{1,0:T(8,128)S(1)}, u32[]{:S(2)}, u32[]{:S(2)}) collective-permute-start(f32[256,1280]{1,0:T(8,128)} %constant_dynamic-update-slice_fusion.refs_0_), channel_id=1, source_target_pairs={{0,4},{4,8},{8,12},{12,0},{1,5},{5,9},{9,13},{13,1},{2,6},{6,10},{... | collective-permute-start | bytes 3932168 | tf_op jit(solution)/shard_map/ppermute | solution.py:25
  53.5 9.6 %collective-permute-start.17 = (f32[4,8,8,512]{3,2,1,0:T(8,128)S(1)}, f32[4,8,8,512]{3,2,1,0:T(8,128)}, u32[]{:S(2)}, u32[]{:S(2)}) collective-permute-start(f32[4,8,8,512]{3,2,1,0:T(8,128)S(1)} %pad_maximum_fusion.own), channel_id=1, source_target_pairs={{0,192},{64,0},{128,64},{192,128},{1,193},{65,1},{129,65},{193,129... | collective-permute-start | bytes 1572872 | tf_op jit(solution)/shard_map/ppermute | solution.py:33
  60.9 9.0 %collective-permute-start.28 = (f32[128,768]{1,0:T(8,128)}, f32[128,768]{1,0:T(8,128)}, u32[]{:S(2)}, u32[]{:S(2)}) collective-permute-start(f32[128,768]{1,0:T(8,128)} %collective-permute-done.27.refs_4_), channel_id=1, source_target_pairs={{0,19},{16,0},{1,16},{17,1},{2,17},{18,2},{3,18},{19,3},{4,23},{20... | collective-permute-start | bytes 1179656 | tf_op jit(solution)/shard_map/ppermute | solution.py:29
  60.9 9.3 %collective-permute-start.25 = (f32[128,768]{1,0:T(8,128)}, f32[128,768]{1,0:T(8,128)}, u32[]{:S(2)}, u32[]{:S(2)}) collective-permute-start(f32[128,768]{1,0:T(8,128)} %collective-permute-done.24.refs_1_), channel_id=1, source_target_pairs={{0,16},{16,1},{1,17},{17,2},{2,18},{18,3},{3,19},{19,0},{4,20},{20... | collective-permute-start | bytes 1179656 | tf_op jit(solution)/shard_map/ppermute | solution.py:29
  63.1 19.0 %collective-permute-start.16 = (f32[4,8,8,512]{3,2,1,0:T(8,128)S(1)}, f32[4,8,8,512]{3,2,1,0:T(8,128)}, u32[]{:S(2)}, u32[]{:S(2)}) collective-permute-start(f32[4,8,8,512]{3,2,1,0:T(8,128)S(1)} %pad_maximum_fusion.own), channel_id=1, source_target_pairs={{0,64},{64,128},{128,192},{192,0},{1,65},{65,129},{129,193},{193,1... | collective-permute-start | bytes 1572872 | tf_op jit(solution)/shard_map/ppermute | solution.py:33
  69.8 21.9 %collective-permute-start.19 = (f32[2,8,8,512]{3,2,1,0:T(8,128)}, f32[2,8,8,512]{3,2,1,0:T(8,128)}, u32[]{:S(2)}, u32[]{:S(2)}) collective-permute-start(f32[2,8,8,512]{3,2,1,0:T(8,128)} %slice.53), channel_id=1, source_target_pairs={{0,192},{64,0},{128,64},{192,128},{1,193},{65,1},{129,65},{193,129... | collective-permute-start | bytes 786440 | tf_op jit(solution)/shard_map/ppermute | solution.py:33
  70.2 15.4 %collective-permute-start.29 = (f32[128,768]{1,0:T(8,128)}, f32[128,768]{1,0:T(8,128)S(1)}, u32[]{:S(2)}, u32[]{:S(2)}) collective-permute-start(f32[128,768]{1,0:T(8,128)} %collective-permute-done.28.refs_5_), channel_id=1, source_target_pairs={{0,19},{16,0},{1,16},{17,1},{2,17},{18,2},{3,18},{19,3},{4,23},{20... | collective-permute-start | bytes 1179656 | tf_op jit(solution)/shard_map/ppermute | solution.py:29
  76.2 12.0 %collective-permute-start.26 = (f32[128,768]{1,0:T(8,128)}, f32[128,768]{1,0:T(8,128)}, u32[]{:S(2)}, u32[]{:S(2)}) collective-permute-start(f32[128,768]{1,0:T(8,128)} %collective-permute-done.25.refs_2_), channel_id=1, source_target_pairs={{0,16},{16,1},{1,17},{17,2},{2,18},{18,3},{3,19},{19,0},{4,20},{20... | collective-permute-start | bytes 1179656 | tf_op jit(solution)/shard_map/ppermute | solution.py:29
  80.9 26.8 %collective-permute-start.11 = (f32[128,1280]{1,0:T(8,128)}, f32[128,1280]{1,0:T(8,128)}, u32[]{:S(2)}, u32[]{:S(2)}) collective-permute-start(f32[128,1280]{1,0:T(8,128)} %slice.51), channel_id=1, source_target_pairs={{0,12},{4,0},{8,4},{12,8},{1,13},{5,1},{9,5},{13,9},{2,14},{6,2},{... | collective-permute-start | bytes 1966088 | tf_op jit(solution)/shard_map/ppermute | solution.py:25
  82.1 25.7 %collective-permute-start.10 = (f32[128,1280]{1,0:T(8,128)}, f32[128,1280]{1,0:T(8,128)}, u32[]{:S(2)}, u32[]{:S(2)}) collective-permute-start(f32[128,1280]{1,0:T(8,128)} %slice.50), channel_id=1, source_target_pairs={{0,4},{4,8},{8,12},{12,0},{1,5},{5,9},{9,13},{13,1},{2,6},{6,10},{... | collective-permute-start | bytes 1966088 | tf_op jit(solution)/shard_map/ppermute | solution.py:25
  85.6 7.0 %collective-permute-start.18 = (f32[2,8,8,512]{3,2,1,0:T(8,128)}, f32[2,8,8,512]{3,2,1,0:T(8,128)}, u32[]{:S(2)}, u32[]{:S(2)}) collective-permute-start(f32[2,8,8,512]{3,2,1,0:T(8,128)} %slice.52), channel_id=1, source_target_pairs={{0,64},{64,128},{128,192},{192,0},{1,65},{65,129},{129,193},{193,1... | collective-permute-start | bytes 786440 | tf_op jit(solution)/shard_map/ppermute | solution.py:33
  88.1 6.5 %collective-permute-start.31 = (f32[64,768]{1,0:T(8,128)S(1)}, f32[64,768]{1,0:T(8,128)S(1)}, u32[]{:S(2)}, u32[]{:S(2)}) collective-permute-start(f32[64,768]{1,0:T(8,128)S(1)} %slice.57), channel_id=1, source_target_pairs={{0,19},{16,0},{1,16},{17,1},{2,17},{18,2},{3,18},{19,3},{4,23},{20... | collective-permute-start | bytes 589832 | tf_op jit(solution)/shard_map/ppermute | solution.py:29
  91.7 7.0 %collective-permute-start.30 = (f32[64,768]{1,0:T(8,128)S(1)}, f32[64,768]{1,0:T(8,128)S(1)}, u32[]{:S(2)}, u32[]{:S(2)}) collective-permute-start(f32[64,768]{1,0:T(8,128)S(1)} %slice.56), channel_id=1, source_target_pairs={{0,16},{16,1},{1,17},{17,2},{2,18},{18,3},{3,19},{19,0},{4,20},{20... | collective-permute-start | bytes 589832 | tf_op jit(solution)/shard_map/ppermute | solution.py:29
  (9 other events, 98.6 us)

commit v2 on v0

v2 whole, which is shorter than its diff:
```python
import functools

import jax
import jax.numpy as jnp
from jax import lax
from jax.experimental import pallas as pl
from jax.experimental.pallas import tpu as pltpu
from jax.sharding import Mesh, PartitionSpec as P

KT = 128
RUN = 16
Z = ("zlo", "zhi")
VMEM = 56 * 2**20
TN = 512


def z_slot(z):
    return (z % 2) * 4 + z // 2


def ring(n, step, slot=lambda i: i):
    return [(slot(i), slot((i + step) % n)) for i in range(n)]


def along_x(a):
    pairs = [(i * 2 + c, (i + 1 - 2 * c) % 4 * 2 + c) for i in range(4) for c in (0, 1)]
    return lax.ppermute(a, ("x", "core"), pairs)


def other_core(a):
    return lax.ppermute(a, "core", [(0, 1), (1, 0)])


def place_of(core, z, y):
    return ((core * 2 + z % 2) * 4 + y) * 4 + z // 2


def cross(a, step, cores=(0, 1), flip=False):
    pairs = []
    for z in range(8):
        for y in range(4):
            for c in cores:
                to = (c, z, (y + step) % 4) if (c == 0) != flip else (c, (z + step) % 8, y)
                pairs.append((place_of(c, z, y), place_of(*to)))
    return lax.ppermute(a, ("core", "zlo", "y", "zhi"), pairs)


def after(a, *others):
    return lax.optimization_barrier((a,) + others)[0]


def split(a):
    h = a.astype(jnp.bfloat16)
    return h, (a - h.astype(jnp.float32)).astype(jnp.bfloat16)


def right_kernel(place, own, near, near_o, far, far_o, mask, hi, lo, rows, *refs):
    parts, sems = refs[:5], refs[5]
    x, core, rep = place[0], place[1], place[2]
    step = 2 * core - 1
    origins = ((x, 0), (x + step, 0), (x - step, 0), (x + 2, 2 * core), (x + 2, 2 - 2 * core))
    sources = (own, near, near_o, far, far_o)
    copies = [pltpu.make_async_copy(a, b, sems.at[i]) for i, (a, b) in enumerate(zip(sources, parts))]
    for copy in copies:
        copy.start()
    for copy, ref, (at_x, first) in zip(copies, parts, origins):
        copy.wait()
        for slot in range(ref.shape[0]):
            base = lax.rem(rep - first - slot + 4, 4) * 32 + lax.rem(at_x + 4, 4) * 8
            for g in range(8):
                rows[pl.ds(pl.multiple_of(g * 128 + base, 8), 8), :] = ref[slot, g]
    for g in range(8):
        at = pl.ds(g * 128, 128)
        hi[at, :], lo[at, :] = split(rows[at, :] * mask[pl.ds(g, 1), :])


def assemble_right(place, sources, mask):
    vm, hbm = pl.BlockSpec(memory_space=pltpu.VMEM), pl.BlockSpec(memory_space=pl.ANY)
    return pl.pallas_call(
        right_kernel,
        out_shape=[jax.ShapeDtypeStruct((1024, 512), jnp.bfloat16)] * 2,
        in_specs=[pl.BlockSpec(memory_space=pltpu.SMEM)] + [hbm] * 5 + [vm],
        out_specs=[vm, vm],
        scratch_shapes=[pltpu.VMEM((1024, 512), jnp.float32)]
        + [pltpu.VMEM(a.shape, jnp.float32) for a in sources]
        + [pltpu.SemaphoreType.DMA((5,))],
        compiler_params=pltpu.CompilerParams(vmem_limit_bytes=VMEM),
    )(place, *sources, mask)


def product_kernel(heights, runs, *refs):
    n = len(heights)
    tiles = 2048 // TN
    pieces, refs = refs[:n], refs[n:]
    mask, hi_in, lo_in, accum, out = refs[:5]
    held, refs = refs[5 : 5 + n], refs[5 + n :]
    hi, lo, lhi, llo, total, piece_sems, in_sems, out_sems, right_sems = refs

    def tile(i):
        return pl.ds(i * TN, TN)

    def fetches(i):
        cols = tile(i)
        copies = [
            pltpu.make_async_copy(a.at[:, cols], b.at[:, cols], piece_sems.at[i, k])
            for k, (a, b) in enumerate(zip(pieces, held))
        ]
        return copies, pltpu.make_async_copy(accum.at[cols], total.at[i], in_sems.at[i])

    right_in = [pltpu.make_async_copy(a, b, right_sems.at[i]) for i, (a, b) in enumerate(((hi_in, hi), (lo_in, lo)))]
    sends = [pltpu.make_async_copy(total.at[i], out.at[tile(i)], out_sems.at[i]) for i in range(tiles)]
    loads = [fetches(i) for i in range(tiles)]
    for copy in loads[0][0] + right_in + [loads[0][1]]:
        copy.start()
    dot = functools.partial(
        lax.dot_general, dimension_numbers=(((0,), (0,)), ((), ())), preferred_element_type=jnp.float32
    )

    def prepare(i):
        cols, slot = tile(i), i % 2
        j = 0
        for ref, height in zip(held, heights):
            for r in range(0, height, RUN):
                run = runs[j]
                there = pl.ds(pl.multiple_of(run * RUN, RUN), RUN)
                a = ref[r : r + RUN, cols] * mask[pl.ds(run // (KT // RUN), 1), cols]
                lhi[slot, there, :], llo[slot, there, :] = split(a)
                j += 1

    for copy in loads[1][0] + [loads[1][1]]:
        copy.start()
    for copy in loads[0][0]:
        copy.wait()
    prepare(0)
    for copy in right_in:
        copy.wait()
    for i in range(tiles):
        if i + 2 < tiles:
            for copy in loads[i + 2][0] + [loads[i + 2][1]]:
                copy.start()
        if i + 1 < tiles:
            for copy in loads[i + 1][0]:
                copy.wait()
        loads[i][1].wait()
        left_hi, left_lo = lhi[i % 2, :1024, :], llo[i % 2, :1024, :]
        add = dot(left_hi, lo[...]) + dot(left_lo, hi[...])
        if i + 1 < tiles:
            prepare(i + 1)
        add = add + dot(left_hi, hi[...])
        total[i] = total[i] + add
        sends[i].start()
    for copy in sends:
        copy.wait()


def product(runs, pieces, mask, hi, lo, accum):
    heights = tuple(p.shape[0] for p in pieces)
    width = pieces[0].shape[1]
    depth = sum(heights)
    tiles = width // TN
    vm, hbm = pl.BlockSpec(memory_space=pltpu.VMEM), pl.BlockSpec(memory_space=pl.ANY)
    sems = pltpu.SemaphoreType.DMA
    scratch = [pltpu.VMEM(p.shape, jnp.float32) for p in pieces]
    scratch += [pltpu.VMEM((1024, 512), jnp.bfloat16)] * 2 + [pltpu.VMEM((2, depth, TN), jnp.bfloat16)] * 2
    scratch += [pltpu.VMEM((tiles, TN, 512), jnp.float32), sems((tiles, len(pieces)))]
    scratch += [sems((tiles,)), sems((tiles,)), sems((2,))]
    return pl.pallas_call(
        functools.partial(product_kernel, heights),
        out_shape=jax.ShapeDtypeStruct(accum.shape, jnp.float32),
        in_specs=[pl.BlockSpec(memory_space=pltpu.SMEM)] + [hbm] * len(pieces) + [vm, hbm, hbm, hbm],
        out_specs=hbm,
        scratch_shapes=scratch,
        compiler_params=pltpu.CompilerParams(vmem_limit_bytes=VMEM),
        cost_estimate=pl.CostEstimate(
            flops=2 * 3 * 1024 * width * 512,
            bytes_accessed=depth * width * 4 + width * 512 * 8 + 2**21,
            transcendentals=0,
        ),
    )(runs, *pieces, mask, hi, lo, accum)


def body(left, right, left_mask, right_mask, accum):
    x, core, y = (lax.axis_index(a) for a in ("x", "core", "y"))
    zlo, rep = lax.axis_index("zlo"), lax.axis_index("zhi")
    z = rep * 2 + zlo
    row, col = x * 2 + core, zlo * 4 + y

    zero = core == 0

    def pick(a, b):
        return jnp.where(zero, a, b)

    def join(*parts):
        return jnp.concatenate(parts, 0)

    s1u, s1d = cross(left, 1), cross(left, -1)
    s2u, s2d = cross(s1u, 1), cross(s1d, -1, (1,))

    m1 = join(left, s1u, s1d, s2u)
    u1, d1 = cross(m1, 1, flip=True), cross(m1, -1, flip=True)
    s3u, s3d = cross(s2u, 1, (1,)), cross(s2d, -1, (1,))
    s4 = cross(s3u, 1, (1,))

    layers = []
    for s in range(4):
        owner = (rep + s) % 4
        part = lax.dynamic_slice_in_dim(right, owner * 512, 512, 3)[:, 0]
        layers.append(part if s == 0 else lax.ppermute(part, "zhi", ring(4, s)))

    layers = jnp.stack(layers)
    other = other_core(layers)
    both = jnp.concatenate([pick(layers, other), pick(other, layers)], 2)
    near = along_x(both)
    near_o = other_core(near)
    far = along_x(pick(near[:2], near[2:]))
    far_o = other_core(far)

    m2 = join(s2d, s3u, s3d, s4)
    u2, d2 = cross(pick(u1, m2), 1, flip=True), cross(pick(d1, m2), -1, flip=True)
    u3a, d3b = cross(pick(u2[:64], u1[:64]), 1, flip=True), cross(d2[64:], -1, flip=True)
    u3b, d3a = cross(pick(u2[64:], u2[:64]), 1, flip=True), cross(pick(d2[:64], d1[64:]), -1, flip=True)

    def run(dy, dz, half):
        yy, zz = (y + dy) % 4, (z + dz) % 8
        return (((zz % 2) * 4 + yy) * 4 + zz // 2) * 2 + half

    def table(core0, core1):
        at, spare = [], [64, 64]
        for pair in zip(core0, core1, strict=True):
            both_at = []
            for c, offsets in enumerate(pair):
                both_at.append(spare[c] if offsets is None else run(*offsets))
                spare[c] += offsets is None
            at.append(pick(*both_at))
        return jnp.stack(at).astype(jnp.int32)

    def halves(*offsets):
        return [(dy, dz, half) for dy, dz in offsets for half in (0, 1)]

    none = [None, None]
    ones, twos, dys = (0, -1, 1, -2), (2, -3, 3, 4), (0, -1, 1, 2)

    def around_z(dz):
        return halves(*((dy, dz) for dy in dys))

    def around_y(dy, dzs):
        return halves(*((dy, dz) for dz in dzs))

    runs = table(
        halves((0, 0), (-1, 0), (1, 0), (2, 0))
        + none * 4
        + around_z(-1)
        + around_z(1)
        + around_z(-2)
        + around_z(2)
        + around_z(-3)
        + around_z(3)
        + around_z(4),
        halves(*((0, dz) for dz in ones + twos))
        + around_y(-1, ones)
        + around_y(1, ones)
        + around_y(-1, twos)
        + around_y(1, twos)
        + around_y(2, ones)[:4]
        + around_y(2, twos)[:4]
        + around_y(2, ones)[4:]
        + around_y(2, twos)[4:]
        + none * 4,
    )

    right_tiles = lax.dynamic_slice(right_mask, (0, col * 16 + rep * 4), (8, 4)).astype(jnp.float32)
    place = jnp.stack([x, core, rep]).astype(jnp.int32)
    right_mask = jnp.repeat(right_tiles, KT, axis=1)
    left_tiles = lax.dynamic_slice(left_mask, (0, row * 16), (8, 16)).astype(jnp.float32)
    mask = jnp.pad(jnp.repeat(left_tiles, KT, axis=1), ((0, 8), (0, 0)))

    u4, d4 = cross(u3a, 1, (0,), True), cross(d3b, -1, (0,), True)
    hi, lo = assemble_right(after(place, u1, d1), [both, near, near_o, far, far_o], right_mask)
    pieces = [left, s1u, s1d, s2u, s2d, s3u, s3d, s4, u1, d1, u2, d2, u3a, u3b, d3a, d3b, u4, d4]
    return product(runs, pieces, mask, hi, lo, accum)


def solution(mesh):
    fine = Mesh(mesh.devices.reshape(4, 2, 2, 4, 4), ("x", "core", "zlo", "y", "zhi"))
    row, col, rep = ("x", "core"), ("zlo", "y"), ("zhi",)
    return jax.shard_map(
        body,
        mesh=fine,
        in_specs=(P(col + rep, row), P(None, rep, row, col), P(), P(), P(row, col + rep)),
        out_specs=P(row, col + rep),
        check_vma=False,
    )
```

time: 317 us -> 105 us (0.33)
  the two profiles are of different devices: /device:TPU:38 before, /device:TPU:1 now
where the time goes in v2:
time: 105 us
  starting transfers between devices  43.9 us (42%)
  waiting for transfers between devices  29 us (28%)
  Pallas kernels  18.4 us (18%)
  local copies, waits for them, and re-layouts  8.93 us (9%)
  other arithmetic  3.48 us (3%)
  between operations  1.12 us (1%)
    ppermute x17, starting transfers between devices, cross(): return lax.ppermute(a, ('core', 'zlo', 'y', 'zhi'), pairs)  30.2 us
    ppermute x17, waiting for transfers between devices, cross(): return lax.ppermute(a, ('core', 'zlo', 'y', 'zhi'), pairs)  22.9 us
    pallas_call x1, Pallas kernels, product(): pl.pallas_call(functools.partial(product_kernel, heights), out_shape=jax....  14.3 us
    ppermute x3, starting transfers between devices, body(): layers.append(part if s == 0 else lax.ppermute(part, 'zhi', ring(4, s)))  6.44 us
    ppermute x2, waiting for transfers between devices, along_x(): return lax.ppermute(a, ('x', 'core'), pairs)  6.13 us
    ppermute x2, starting transfers between devices, along_x(): return lax.ppermute(a, ('x', 'core'), pairs)  6.04 us
    unnamed x44, local copies, waits for them, and re-layouts  4.83 us
    pallas_call x1, Pallas kernels, assemble_right(): pl.pallas_call(right_kernel, out_shape=[jax.ShapeDtypeStruct((1024, 512),...  4.12 us
  transfers between devices with their start and end apart: 25, of which 7 were waited for; matrix products, arithmetic and copies ran while one was open for 10% of the time, Pallas kernels for 4%

profile of v2, /device:TPU:1, one launch (start us, length us, event | category | flops | bytes accessed | tf_op | source)
XLA Modules:
  0.0 104.9 jit_solution(4043629998030916918)
XLA Ops:
  0.0 6.4 %collective-permute-start.1 = (f32[32,2048]{1,0:T(8,128)}, f32[32,2048]{1,0:T(8,128)S(1)}, u32[]{:S(2)}, u32[]{:S(2)}) collective-permute-start(f32[32,2048]{1,0:T(8,128)} %refs_0_.1), channel_id=1, source_target_pairs={{0,12},{32,51},{4,0},{36,55},{8,4},{40,59},{12,8},{44,63},{16,28},... | collective-permute-start | bytes 786440 | tf_op jit(solution)/shard_map/ppermute | solution.py:45
  6.4 1.0 dynamic-slice_bitcast_fusion.3
  7.5 3.6 %collective-permute-start.19 = (f32[8,4,512]{2,1,0:T(4,128)S(1)}, f32[8,4,512]{2,1,0:T(4,128)S(1)}, u32[]{:S(2)}, u32[]{:S(2)}) collective-permute-start(f32[8,4,512]{2,1,0:T(4,128)S(1)} %get-tuple-element.21), channel_id=1, source_target_pairs={{0,3},{1,0},{2,1},{3,2},{4,7},{5,4},{6,5},{7,6},{8,11},{9,8},{10,9... | collective-permute-start | bytes 196616 | tf_op jit(solution)/shard_map/ppermute | solution.py:208
  11.0 2.8 %collective-permute-start.18 = (f32[8,4,512]{2,1,0:T(4,128)S(1)}, f32[8,4,512]{2,1,0:T(4,128)S(1)}, u32[]{:S(2)}, u32[]{:S(2)}) collective-permute-start(f32[8,4,512]{2,1,0:T(4,128)S(1)} %get-tuple-element.22), channel_id=1, source_target_pairs={{0,2},{1,3},{2,0},{3,1},{4,6},{5,7},{6,4},{7,5},{8,10},{9,11},{10,... | collective-permute-start | bytes 196616 | tf_op jit(solution)/shard_map/ppermute | solution.py:208
  13.8 1.7 %constant_dynamic-update-slice_fusion.3 = f32[128,2048]{1,0:T(8,128)} fusion(f32[32,2048]{1,0:T(8,128)} %refs_0_.1), kind=kLoop, calls=%fused_computation.18 | loop fusion | bytes 524288
  15.5 1.9 %collective-permute-start.3 = (f32[32,2048]{1,0:T(8,128)S(1)}, f32[32,2048]{1,0:T(8,128)S(1)}, u32[]{:S(2)}, u32[]{:S(2)}) collective-permute-start(f32[32,2048]{1,0:T(8,128)S(1)} %collective-permute-done.1.refs_2_), channel_id=1, source_target_pairs={{32,51},{36,55},{40,59},{44,63},{48,32},{52,36},{56,40},{60,44},{3... | collective-permute-start | bytes 786440 | tf_op jit(solution)/shard_map/ppermute | solution.py:45
  17.4 1.5 %collective-permute-start.2 = (f32[32,2048]{1,0:T(8,128)S(1)}, f32[32,2048]{1,0:T(8,128)S(1)}, u32[]{:S(2)}, u32[]{:S(2)}) collective-permute-start(f32[32,2048]{1,0:T(8,128)S(1)} %collective-permute-done.refs_1_), channel_id=1, source_target_pairs={{0,4},{32,48},{4,8},{36,52},{8,12},{40,56},{12,0},{44,60},{16,20},... | collective-permute-start | bytes 786440 | tf_op jit(solution)/shard_map/ppermute | solution.py:45
  19.0 0.7 constant_dynamic-update-slice_fusion.2
  20.4 3.8 %collective-permute-done.2.refs_3_ = f32[32,2048]{1,0:T(8,128)S(1)} collective-permute-done((f32[32,2048]{1,0:T(8,128)S(1)}, f32[32,2048]{1,0:T(8,128)S(1)}, u32[]{:S(2)}, u32[]{:S(2)}) %collective-permute-start.2) | collective-permute-done | bytes 262176 | tf_op jit(solution)/shard_map/ppermute | solution.py:45
  24.2 0.8 constant_dynamic-update-slice_fusion
  25.0 2.4 %collective-permute-start.8 = (f32[128,2048]{1,0:T(8,128)}, f32[128,2048]{1,0:T(8,128)S(1)}, u32[]{:S(2)}, u32[]{:S(2)}) collective-permute-start(f32[128,2048]{1,0:T(8,128)} %constant_dynamic-update-slice_fusion), channel_id=1, source_target_pairs={{0,19},{32,44},{4,23},{36,32},{8,27},{40,36},{12,31},{44,40},{16,0... | collective-permute-start | bytes 3145736 | tf_op jit(solution)/shard_map/ppermute | solution.py:45
  27.4 2.4 %collective-permute-start.4 = (f32[32,2048]{1,0:T(8,128)S(1)}, f32[32,2048]{1,0:T(8,128)S(1)}, u32[]{:S(2)}, u32[]{:S(2)}) collective-permute-start(f32[32,2048]{1,0:T(8,128)S(1)} %collective-permute-done.2.refs_3_), channel_id=1, source_target_pairs={{32,48},{36,52},{40,56},{44,60},{48,33},{52,37},{56,41},{60,45},{3... | collective-permute-start | bytes 786440 | tf_op jit(solution)/shard_map/ppermute | solution.py:45
  30.6 3.6 %collective-permute-start.5 = (f32[32,2048]{1,0:T(8,128)S(1)}, f32[32,2048]{1,0:T(8,128)S(1)}, u32[]{:S(2)}, u32[]{:S(2)}) collective-permute-start(f32[32,2048]{1,0:T(8,128)S(1)} %collective-permute-done.3.refs_4_), channel_id=1, source_target_pairs={{32,51},{36,55},{40,59},{44,63},{48,32},{52,36},{56,40},{60,44},{3... | collective-permute-start | bytes 786440 | tf_op jit(solution)/shard_map/ppermute | solution.py:45
  34.2 4.7 %collective-permute-done.4.refs_5_ = f32[32,2048]{1,0:T(8,128)S(1)} collective-permute-done((f32[32,2048]{1,0:T(8,128)S(1)}, f32[32,2048]{1,0:T(8,128)S(1)}, u32[]{:S(2)}, u32[]{:S(2)}) %collective-permute-start.4) | collective-permute-done | bytes 262176 | tf_op jit(solution)/shard_map/ppermute | solution.py:45
  38.9 1.9 %collective-permute-start.6 = (f32[32,2048]{1,0:T(8,128)S(1)}, f32[32,2048]{1,0:T(8,128)S(1)}, u32[]{:S(2)}, u32[]{:S(2)}) collective-permute-start(f32[32,2048]{1,0:T(8,128)S(1)} %collective-permute-done.4.refs_5_), channel_id=1, source_target_pairs={{32,48},{36,52},{40,56},{44,60},{48,33},{52,37},{56,41},{60,45},{3... | collective-permute-start | bytes 786440 | tf_op jit(solution)/shard_map/ppermute | solution.py:45
  40.9 8.0 %collective-permute-done.6.refs_7_ = f32[32,2048]{1,0:T(8,128)S(1)} collective-permute-done((f32[32,2048]{1,0:T(8,128)S(1)}, f32[32,2048]{1,0:T(8,128)S(1)}, u32[]{:S(2)}, u32[]{:S(2)}) %collective-permute-start.6) | collective-permute-done | bytes 262176 | tf_op jit(solution)/shard_map/ppermute | solution.py:45
  49.8 1.8 %collective-permute-start.10 = (f32[128,2048]{1,0:T(8,128)S(1)}, f32[128,2048]{1,0:T(8,128)S(1)}, u32[]{:S(2)}, u32[]{:S(2)}) collective-permute-start(f32[128,2048]{1,0:T(8,128)S(1)} %get-tuple-element.15), channel_id=1, source_target_pairs={{0,19},{32,44},{4,23},{36,32},{8,27},{40,36},{12,31},{44,40},{16,0... | collective-permute-start | bytes 3145736 | tf_op jit(solution)/shard_map/ppermute | solution.py:45
  51.9 2.6 %collective-permute-start.21 = (f32[4,8,8,512]{3,2,1,0:T(8,128)S(1)}, f32[4,8,8,512]{3,2,1,0:T(8,128)S(1)}, u32[]{:S(2)}, u32[]{:S(2)}) collective-permute-start(f32[4,8,8,512]{3,2,1,0:T(8,128)S(1)} %pad_maximum_fusion.own), channel_id=1, source_target_pairs={{0,64},{32,224},{64,128},{96,32},{128,192},{160,96},{192,0},{224,1... | collective-permute-start | bytes 1572872 | tf_op jit(solution)/shard_map/ppermute | solution.py:27
  54.5 6.1 %collective-permute-done.21.near = f32[4,8,8,512]{3,2,1,0:T(8,128)S(1)} collective-permute-done((f32[4,8,8,512]{3,2,1,0:T(8,128)S(1)}, f32[4,8,8,512]{3,2,1,0:T(8,128)S(1)}, u32[]{:S(2)}, u32[]{:S(2)}) %collective-permute-start.21) | collective-permute-done | bytes 524320 | tf_op jit(solution)/shard_map/ppermute | solution.py:27
  60.6 3.5 %collective-permute-start.23 = (f32[2,8,8,512]{3,2,1,0:T(8,128)S(1)}, f32[2,8,8,512]{3,2,1,0:T(8,128)S(1)}, u32[]{:S(2)}, u32[]{:S(2)}) collective-permute-start(f32[2,8,8,512]{3,2,1,0:T(8,128)S(1)} %slice_select_fusion.3), channel_id=1, source_target_pairs={{0,64},{32,224},{64,128},{96,32},{128,192},{160,96},{192,0},{224,1... | collective-permute-start | bytes 786440 | tf_op jit(solution)/shard_map/ppermute | solution.py:27
  64.1 1.2 %fusion = (f32[64,2048]{1,0:T(8,128)}, f32[64,2048]{1,0:T(8,128)}) fusion(f32[128,2048]{1,0:T(8,128)S(1)} %collective-permute-done.10.refs_11_, f32[128,2048]{1,0:T(8,128)S(1)} %collective-permute-done.8.refs_9_, pred[]{:T(512)S(6)} %eq.392), kind=kLoop, calls=%fused_computation.27 | loop fusion | flops 131072 | bytes 2621441 | tf_op jit(solution)/shard_map/slice | solution.py:220
  65.3 2.6 %collective-permute-start.14 = (f32[64,2048]{1,0:T(8,128)}, f32[64,2048]{1,0:T(8,128)}, u32[]{:S(2)}, u32[]{:S(2)}) collective-permute-start(f32[64,2048]{1,0:T(8,128)} %get-tuple-element.11), channel_id=1, source_target_pairs={{0,19},{32,44},{4,23},{36,32},{8,27},{40,36},{12,31},{44,40},{16,0... | collective-permute-start | bytes 1572872 | tf_op jit(solution)/shard_map/ppermute | solution.py:45
  68.0 1.3 %collective-permute-done.9.refs_10_ = f32[128,2048]{1,0:T(8,128)S(1)} collective-permute-done((f32[128,2048]{1,0:T(8,128)S(1)}, f32[128,2048]{1,0:T(8,128)S(1)}, u32[]{:S(2)}, u32[]{:S(2)}) %collective-permute-start.9) | collective-permute-done | bytes 1048608 | tf_op jit(solution)/shard_map/ppermute | solution.py:45
  69.3 1.0 slice_select_fusion.1
  71.2 2.6 %collective-permute-start.13 = (f32[64,2048]{1,0:T(8,128)}, f32[64,2048]{1,0:T(8,128)}, u32[]{:S(2)}, u32[]{:S(2)}) collective-permute-start(f32[64,2048]{1,0:T(8,128)} %get-tuple-element.12), channel_id=1, source_target_pairs={{0,19},{32,44},{4,23},{36,32},{8,27},{40,36},{12,31},{44,40},{16,0... | collective-permute-start | bytes 1572872 | tf_op jit(solution)/shard_map/ppermute | solution.py:45
  74.4 1.5 %collective-permute-start.16 = (f32[64,2048]{1,0:T(8,128)}, f32[64,2048]{1,0:T(8,128)}, u32[]{:S(2)}, u32[]{:S(2)}) collective-permute-start(f32[64,2048]{1,0:T(8,128)} %collective-permute-done.14.refs_15_), channel_id=1, source_target_pairs={{0,19},{4,23},{8,27},{12,31},{16,0},{20,4},{24,8},{28,12},{1,16},{... | collective-permute-start | bytes 1572872 | tf_op jit(solution)/shard_map/ppermute | solution.py:45
  75.9 4.4 %collective-permute-done.11.refs_12_ = f32[64,2048]{1,0:T(8,128)S(1)} collective-permute-done((f32[64,2048]{1,0:T(8,128)}, f32[64,2048]{1,0:T(8,128)S(1)}, u32[]{:S(2)}, u32[]{:S(2)}) %collective-permute-start.11) | collective-permute-done | bytes 524320 | tf_op jit(solution)/shard_map/ppermute | solution.py:45
  80.3 1.5 %collective-permute-start.15 = (f32[64,2048]{1,0:T(8,128)S(1)}, f32[64,2048]{1,0:T(8,128)}, u32[]{:S(2)}, u32[]{:S(2)}) collective-permute-start(f32[64,2048]{1,0:T(8,128)S(1)} %collective-permute-done.11.refs_12_), channel_id=1, source_target_pairs={{0,16},{4,20},{8,24},{12,28},{16,1},{20,5},{24,9},{28,13},{1,17},{... | collective-permute-start | bytes 1572872 | tf_op jit(solution)/shard_map/ppermute | solution.py:45
  83.3 0.8 stack.315.runs
  85.4 0.8 copy-done.6
  86.2 4.1 %shard_map.55 = (bf16[1024,512]{1,0:T(8,128)(2,1)}, bf16[1024,512]{1,0:T(8,128)(2,1)}) custom-call(s32[3]{0:T(128)} %pad_add_fusion.place, f32[4,8,8,512]{3,2,1,0:T(8,128)} %copy-done.2, f32[4,8,8,512]{3,2,1,0:T(8,128)} %copy-done.3, f32[4,8,8,512]{3,2,1,0:T(8,128)} %copy-done.6, f32[2,8,8,512]{3,2,1,0:T(8,128)} %copy-done.7, f32[2,8,8,512]{3,2,1,0:T(8,128)} %copy-done.8, ...), custom_call_target="tpu_custom_call" | custom-call | tf_op jit(solution)/shard_map/pallas_call | solution.py:79
  90.4 14.3 %shard_map.56 = f32[2048,512]{1,0:T(8,128)} custom-call(s32[72]{0:T(128)} %stack.315.runs, f32[32,2048]{1,0:T(8,128)} %refs_0_.1, f32[32,2048]{1,0:T(8,128)} %copy-done.10, f32[32,2048]{1,0:T(8,128)} %copy-done.9, f32[32,2048]{1,0:T(8,128)} %copy-done.12, f32[32,2048]{1,0:T(8,128)} %copy-done.11, f32[32,2048]{1,0:T(8,128)} %copy-done.13, ...), custom_call_target="tpu_custom_call" | custom-call | flops 6442450944 | bytes 19922944 | tf_op jit(solution)/shard_map/pallas_call | solution.py:167
  (83 shorter events, 6.4 us)
Async XLA Ops:
  0.0 15.5 %collective-permute-start.1 = (f32[32,2048]{1,0:T(8,128)}, f32[32,2048]{1,0:T(8,128)S(1)}, u32[]{:S(2)}, u32[]{:S(2)}) collective-permute-start(f32[32,2048]{1,0:T(8,128)} %refs_0_.1), channel_id=1, source_target_pairs={{0,12},{32,51},{4,0},{36,55},{8,4},{40,59},{12,8},{44,63},{16,28},... | collective-permute-start | bytes 786440 | tf_op jit(solution)/shard_map/ppermute | solution.py:45
  6.4 11.0 %collective-permute-start = (f32[32,2048]{1,0:T(8,128)}, f32[32,2048]{1,0:T(8,128)S(1)}, u32[]{:S(2)}, u32[]{:S(2)}) collective-permute-start(f32[32,2048]{1,0:T(8,128)} %refs_0_.1), channel_id=1, source_target_pairs={{0,4},{32,48},{4,8},{36,52},{8,12},{40,56},{12,0},{44,60},{16,20},... | collective-permute-start | bytes 786440 | tf_op jit(solution)/shard_map/ppermute | solution.py:45
  7.4 20.1 %collective-permute-start.17 = (f32[8,4,512]{2,1,0:T(4,128)S(1)}, f32[8,4,512]{2,1,0:T(4,128)S(1)}, u32[]{:S(2)}, u32[]{:S(2)}) collective-permute-start(f32[8,4,512]{2,1,0:T(4,128)S(1)} %get-tuple-element.20), channel_id=1, source_target_pairs={{0,1},{1,2},{2,3},{3,0},{4,5},{5,6},{6,7},{7,4},{8,9},{9,10},{10,1... | collective-permute-start | bytes 196616 | tf_op jit(solution)/shard_map/ppermute | solution.py:208
  7.5 20.0 %collective-permute-start.19 = (f32[8,4,512]{2,1,0:T(4,128)S(1)}, f32[8,4,512]{2,1,0:T(4,128)S(1)}, u32[]{:S(2)}, u32[]{:S(2)}) collective-permute-start(f32[8,4,512]{2,1,0:T(4,128)S(1)} %get-tuple-element.21), channel_id=1, source_target_pairs={{0,3},{1,0},{2,1},{3,2},{4,7},{5,4},{6,5},{7,6},{8,11},{9,8},{10,9... | collective-permute-start | bytes 196616 | tf_op jit(solution)/shard_map/ppermute | solution.py:208
  11.0 18.9 %collective-permute-start.18 = (f32[8,4,512]{2,1,0:T(4,128)S(1)}, f32[8,4,512]{2,1,0:T(4,128)S(1)}, u32[]{:S(2)}, u32[]{:S(2)}) collective-permute-start(f32[8,4,512]{2,1,0:T(4,128)S(1)} %get-tuple-element.22), channel_id=1, source_target_pairs={{0,2},{1,3},{2,0},{3,1},{4,6},{5,7},{6,4},{7,5},{8,10},{9,11},{10,... | collective-permute-start | bytes 196616 | tf_op jit(solution)/shard_map/ppermute | solution.py:208
  15.5 34.3 %copy-start.9 = (f32[32,2048]{1,0:T(8,128)}, f32[32,2048]{1,0:T(8,128)S(1)}, u32[]{:S(2)}) copy-start(f32[32,2048]{1,0:T(8,128)S(1)} %collective-permute-done.1.refs_2_) | copy-start | bytes 786436
  15.5 15.1 %collective-permute-start.3 = (f32[32,2048]{1,0:T(8,128)S(1)}, f32[32,2048]{1,0:T(8,128)S(1)}, u32[]{:S(2)}, u32[]{:S(2)}) collective-permute-start(f32[32,2048]{1,0:T(8,128)S(1)} %collective-permute-done.1.refs_2_), channel_id=1, source_target_pairs={{32,51},{36,55},{40,59},{44,63},{48,32},{52,36},{56,40},{60,44},{3... | collective-permute-start | bytes 786440 | tf_op jit(solution)/shard_map/ppermute | solution.py:45
  17.4 6.8 %collective-permute-start.2 = (f32[32,2048]{1,0:T(8,128)S(1)}, f32[32,2048]{1,0:T(8,128)S(1)}, u32[]{:S(2)}, u32[]{:S(2)}) collective-permute-start(f32[32,2048]{1,0:T(8,128)S(1)} %collective-permute-done.refs_1_), channel_id=1, source_target_pairs={{0,4},{32,48},{4,8},{36,52},{8,12},{40,56},{12,0},{44,60},{16,20},... | collective-permute-start | bytes 786440 | tf_op jit(solution)/shard_map/ppermute | solution.py:45
  24.2 25.5 %copy-start.12 = (f32[32,2048]{1,0:T(8,128)}, f32[32,2048]{1,0:T(8,128)S(1)}, u32[]{:S(2)}) copy-start(f32[32,2048]{1,0:T(8,128)S(1)} %collective-permute-done.2.refs_3_) | copy-start | bytes 786436
  25.0 23.9 %collective-permute-start.8 = (f32[128,2048]{1,0:T(8,128)}, f32[128,2048]{1,0:T(8,128)S(1)}, u32[]{:S(2)}, u32[]{:S(2)}) collective-permute-start(f32[128,2048]{1,0:T(8,128)} %constant_dynamic-update-slice_fusion), channel_id=1, source_target_pairs={{0,19},{32,44},{4,23},{36,32},{8,27},{40,36},{12,31},{44,40},{16,0... | collective-permute-start | bytes 3145736 | tf_op jit(solution)/shard_map/ppermute | solution.py:45
  27.4 22.1 %collective-permute-start.7 = (f32[128,2048]{1,0:T(8,128)}, f32[128,2048]{1,0:T(8,128)S(1)}, u32[]{:S(2)}, u32[]{:S(2)}) collective-permute-start(f32[128,2048]{1,0:T(8,128)} %constant_dynamic-update-slice_fusion), channel_id=1, source_target_pairs={{0,16},{32,36},{4,20},{36,40},{8,24},{40,44},{12,28},{44,32},{16,1... | collective-permute-start | bytes 3145736 | tf_op jit(solution)/shard_map/ppermute | solution.py:45
  27.4 11.4 %collective-permute-start.4 = (f32[32,2048]{1,0:T(8,128)S(1)}, f32[32,2048]{1,0:T(8,128)S(1)}, u32[]{:S(2)}, u32[]{:S(2)}) collective-permute-start(f32[32,2048]{1,0:T(8,128)S(1)} %collective-permute-done.2.refs_3_), channel_id=1, source_target_pairs={{32,48},{36,52},{40,56},{44,60},{48,33},{52,37},{56,41},{60,45},{3... | collective-permute-start | bytes 786440 | tf_op jit(solution)/shard_map/ppermute | solution.py:45
  30.0 21.6 %collective-permute-start.20 = (f32[4,8,4,512]{3,2,1,0:T(4,128)S(1)}, f32[4,8,4,512]{3,2,1,0:T(4,128)S(1)}, u32[]{:S(2)}, u32[]{:S(2)}) collective-permute-start(f32[4,8,4,512]{3,2,1,0:T(4,128)S(1)} %pad_maximum_fusion.1), channel_id=1, source_target_pairs={{0,32},{32,0},{1,33},{33,1},{2,34},{34,2},{3,35},{35,3},{4,36},{36... | collective-permute-start | bytes 786440 | tf_op jit(solution)/shard_map/ppermute | solution.py:31
  30.6 21.2 %copy-start.11 = (f32[32,2048]{1,0:T(8,128)}, f32[32,2048]{1,0:T(8,128)S(1)}, u32[]{:S(2)}) copy-start(f32[32,2048]{1,0:T(8,128)S(1)} %collective-permute-done.3.refs_4_) | copy-start | bytes 786436
  30.6 10.3 %collective-permute-start.5 = (f32[32,2048]{1,0:T(8,128)S(1)}, f32[32,2048]{1,0:T(8,128)S(1)}, u32[]{:S(2)}, u32[]{:S(2)}) collective-permute-start(f32[32,2048]{1,0:T(8,128)S(1)} %collective-permute-done.3.refs_4_), channel_id=1, source_target_pairs={{32,51},{36,55},{40,59},{44,63},{48,32},{52,36},{56,40},{60,44},{3... | collective-permute-start | bytes 786440 | tf_op jit(solution)/shard_map/ppermute | solution.py:45
  38.9 10.0 %collective-permute-start.6 = (f32[32,2048]{1,0:T(8,128)S(1)}, f32[32,2048]{1,0:T(8,128)S(1)}, u32[]{:S(2)}, u32[]{:S(2)}) collective-permute-start(f32[32,2048]{1,0:T(8,128)S(1)} %collective-permute-done.4.refs_5_), channel_id=1, source_target_pairs={{32,48},{36,52},{40,56},{44,60},{48,33},{52,37},{56,41},{60,45},{3... | collective-permute-start | bytes 786440 | tf_op jit(solution)/shard_map/ppermute | solution.py:45
  49.8 20.8 %copy-start.16 = (s32[8,128]{1,0:T(8,128)S(1)}, s32[8,128]{1,0:T(8,128)}, u32[]{:S(2)}) copy-start(s32[8,128]{1,0:T(8,128)} %param.7) | copy-start | bytes 12292
  49.8 14.3 %collective-permute-start.10 = (f32[128,2048]{1,0:T(8,128)S(1)}, f32[128,2048]{1,0:T(8,128)S(1)}, u32[]{:S(2)}, u32[]{:S(2)}) collective-permute-start(f32[128,2048]{1,0:T(8,128)S(1)} %get-tuple-element.15), channel_id=1, source_target_pairs={{0,19},{32,44},{4,23},{36,32},{8,27},{40,36},{12,31},{44,40},{16,0... | collective-permute-start | bytes 3145736 | tf_op jit(solution)/shard_map/ppermute | solution.py:45
  51.8 30.7 %copy-start.17 = (s32[8,128]{1,0:T(8,128)S(1)}, s32[8,128]{1,0:T(8,128)}, u32[]{:S(2)}) copy-start(s32[8,128]{1,0:T(8,128)} %param.8) | copy-start | bytes 12292
  51.9 33.5 %copy-start.2 = (f32[4,8,8,512]{3,2,1,0:T(8,128)}, f32[4,8,8,512]{3,2,1,0:T(8,128)S(1)}, u32[]{:S(2)}) copy-start(f32[4,8,8,512]{3,2,1,0:T(8,128)S(1)} %pad_maximum_fusion.own) | copy-start | bytes 1572868
  51.9 8.7 %collective-permute-start.21 = (f32[4,8,8,512]{3,2,1,0:T(8,128)S(1)}, f32[4,8,8,512]{3,2,1,0:T(8,128)S(1)}, u32[]{:S(2)}, u32[]{:S(2)}) collective-permute-start(f32[4,8,8,512]{3,2,1,0:T(8,128)S(1)} %pad_maximum_fusion.own), channel_id=1, source_target_pairs={{0,64},{32,224},{64,128},{96,32},{128,192},{160,96},{192,0},{224,1... | collective-permute-start | bytes 1572872 | tf_op jit(solution)/shard_map/ppermute | solution.py:27
  54.5 14.9 %collective-permute-start.9 = (f32[128,2048]{1,0:T(8,128)S(1)}, f32[128,2048]{1,0:T(8,128)S(1)}, u32[]{:S(2)}, u32[]{:S(2)}) collective-permute-start(f32[128,2048]{1,0:T(8,128)S(1)} %get-tuple-element.16), channel_id=1, source_target_pairs={{0,16},{32,36},{4,20},{36,40},{8,24},{40,44},{12,28},{44,32},{16,1... | collective-permute-start | bytes 3145736 | tf_op jit(solution)/shard_map/ppermute | solution.py:45
  60.6 24.8 %copy-start.3 = (f32[4,8,8,512]{3,2,1,0:T(8,128)}, f32[4,8,8,512]{3,2,1,0:T(8,128)S(1)}, u32[]{:S(2)}) copy-start(f32[4,8,8,512]{3,2,1,0:T(8,128)S(1)} %collective-permute-done.21.near) | copy-start | bytes 1572868
  60.6 9.9 %collective-permute-start.23 = (f32[2,8,8,512]{3,2,1,0:T(8,128)S(1)}, f32[2,8,8,512]{3,2,1,0:T(8,128)S(1)}, u32[]{:S(2)}, u32[]{:S(2)}) collective-permute-start(f32[2,8,8,512]{3,2,1,0:T(8,128)S(1)} %slice_select_fusion.3), channel_id=1, source_target_pairs={{0,64},{32,224},{64,128},{96,32},{128,192},{160,96},{192,0},{224,1... | collective-permute-start | bytes 786440 | tf_op jit(solution)/shard_map/ppermute | solution.py:27
  65.3 9.1 %collective-permute-start.14 = (f32[64,2048]{1,0:T(8,128)}, f32[64,2048]{1,0:T(8,128)}, u32[]{:S(2)}, u32[]{:S(2)}) collective-permute-start(f32[64,2048]{1,0:T(8,128)} %get-tuple-element.11), channel_id=1, source_target_pairs={{0,19},{32,44},{4,23},{36,32},{8,27},{40,36},{12,31},{44,40},{16,0... | collective-permute-start | bytes 1572872 | tf_op jit(solution)/shard_map/ppermute | solution.py:45
  70.5 9.9 %collective-permute-start.11 = (f32[64,2048]{1,0:T(8,128)}, f32[64,2048]{1,0:T(8,128)S(1)}, u32[]{:S(2)}, u32[]{:S(2)}) collective-permute-start(f32[64,2048]{1,0:T(8,128)} %get-tuple-element.14), channel_id=1, source_target_pairs={{0,16},{32,36},{4,20},{36,40},{8,24},{40,44},{12,28},{44,32},{16,1... | collective-permute-start | bytes 1572872 | tf_op jit(solution)/shard_map/ppermute | solution.py:45
  70.5 3.3 %collective-permute-start.24 = (f32[2,8,8,512]{3,2,1,0:T(8,128)S(1)}, f32[2,8,8,512]{3,2,1,0:T(8,128)S(1)}, u32[]{:S(2)}, u32[]{:S(2)}) collective-permute-start(f32[2,8,8,512]{3,2,1,0:T(8,128)S(1)} %collective-permute-done.23.far), channel_id=1, source_target_pairs={{0,32},{32,0},{1,33},{33,1},{2,34},{34,2},{3,35},{35,3},{4,36},{36... | collective-permute-start | bytes 786440 | tf_op jit(solution)/shard_map/ppermute | solution.py:31
  70.8 14.6 %collective-permute-start.22 = (f32[4,8,8,512]{3,2,1,0:T(8,128)S(1)}, f32[4,8,8,512]{3,2,1,0:T(8,128)S(1)}, u32[]{:S(2)}, u32[]{:S(2)}) collective-permute-start(f32[4,8,8,512]{3,2,1,0:T(8,128)S(1)} %collective-permute-done.21.near), channel_id=1, source_target_pairs={{0,32},{32,0},{1,33},{33,1},{2,34},{34,2},{3,35},{35,3},{4,36},{36... | collective-permute-start | bytes 1572872 | tf_op jit(solution)/shard_map/ppermute | solution.py:31
  71.2 19.1 %collective-permute-start.13 = (f32[64,2048]{1,0:T(8,128)}, f32[64,2048]{1,0:T(8,128)}, u32[]{:S(2)}, u32[]{:S(2)}) collective-permute-start(f32[64,2048]{1,0:T(8,128)} %get-tuple-element.12), channel_id=1, source_target_pairs={{0,19},{32,44},{4,23},{36,32},{8,27},{40,36},{12,31},{44,40},{16,0... | collective-permute-start | bytes 1572872 | tf_op jit(solution)/shard_map/ppermute | solution.py:45
  73.8 16.5 %collective-permute-start.12 = (f32[64,2048]{1,0:T(8,128)S(1)}, f32[64,2048]{1,0:T(8,128)}, u32[]{:S(2)}, u32[]{:S(2)}) collective-permute-start(f32[64,2048]{1,0:T(8,128)S(1)} %get-tuple-element.13), channel_id=1, source_target_pairs={{0,16},{32,36},{4,20},{36,40},{8,24},{40,44},{12,28},{44,32},{16,1... | collective-permute-start | bytes 1572872 | tf_op jit(solution)/shard_map/ppermute | solution.py:45
  74.4 15.9 %collective-permute-start.16 = (f32[64,2048]{1,0:T(8,128)}, f32[64,2048]{1,0:T(8,128)}, u32[]{:S(2)}, u32[]{:S(2)}) collective-permute-start(f32[64,2048]{1,0:T(8,128)} %collective-permute-done.14.refs_15_), channel_id=1, source_target_pairs={{0,19},{4,23},{8,27},{12,31},{16,0},{20,4},{24,8},{28,12},{1,16},{... | collective-permute-start | bytes 1572872 | tf_op jit(solution)/shard_map/ppermute | solution.py:45
  80.3 10.0 %collective-permute-start.15 = (f32[64,2048]{1,0:T(8,128)S(1)}, f32[64,2048]{1,0:T(8,128)}, u32[]{:S(2)}, u32[]{:S(2)}) collective-permute-start(f32[64,2048]{1,0:T(8,128)S(1)} %collective-permute-done.11.refs_12_), channel_id=1, source_target_pairs={{0,16},{4,20},{8,24},{12,28},{16,1},{20,5},{24,9},{28,13},{1,17},{... | collective-permute-start | bytes 1572872 | tf_op jit(solution)/shard_map/ppermute | solution.py:45
  (12 other events, 105.8 us)

commit v3 on v2

--- a/solution.py
+++ b/solution.py
@@ -138,15 +138,14 @@
         if i + 2 < tiles:
             for copy in loads[i + 2][0] + [loads[i + 2][1]]:
                 copy.start()
+        left_hi, left_lo = lhi[i % 2, :1024, :], llo[i % 2, :1024, :]
+        add = dot(left_hi, lo[...]) + dot(left_lo, hi[...])
         if i + 1 < tiles:
             for copy in loads[i + 1][0]:
                 copy.wait()
-        loads[i][1].wait()
-        left_hi, left_lo = lhi[i % 2, :1024, :], llo[i % 2, :1024, :]
-        add = dot(left_hi, lo[...]) + dot(left_lo, hi[...])
-        if i + 1 < tiles:
             prepare(i + 1)
         add = add + dot(left_hi, hi[...])
+        loads[i][1].wait()
         total[i] = total[i] + add
         sends[i].start()
     for copy in sends:

time: 105 us -> 105 us (level)
  no operation moved by 1% of the time
where the time goes in v3:
time: 105 us
  starting transfers between devices  43.9 us (42%)
  waiting for transfers between devices  29 us (28%)
  Pallas kernels  18.1 us (17%)
  local copies, waits for them, and re-layouts  8.93 us (9%)
  other arithmetic  3.48 us (3%)
  between operations  1.12 us (1%)
    ppermute x17, starting transfers between devices, cross(): return lax.ppermute(a, ('core', 'zlo', 'y', 'zhi'), pairs)  30.2 us
    ppermute x17, waiting for transfers between devices, cross(): return lax.ppermute(a, ('core', 'zlo', 'y', 'zhi'), pairs)  22.9 us
    pallas_call x1, Pallas kernels, product(): pl.pallas_call(functools.partial(product_kernel, heights), out_shape=jax....  14 us
    ppermute x3, starting transfers between devices, body(): layers.append(part if s == 0 else lax.ppermute(part, 'zhi', ring(4, s)))  6.44 us
    ppermute x2, waiting for transfers between devices, along_x(): return lax.ppermute(a, ('x', 'core'), pairs)  6.13 us
    ppermute x2, starting transfers between devices, along_x(): return lax.ppermute(a, ('x', 'core'), pairs)  6.04 us
    unnamed x44, local copies, waits for them, and re-layouts  4.83 us
    pallas_call x1, Pallas kernels, assemble_right(): pl.pallas_call(right_kernel, out_shape=[jax.ShapeDtypeStruct((1024, 512),...  4.12 us
  transfers between devices with their start and end apart: 25, of which 7 were waited for; matrix products, arithmetic and copies ran while one was open for 10% of the time, Pallas kernels for 4%

profile of v3, /device:TPU:1, one launch (start us, length us, event | category | flops | bytes accessed | tf_op | source)
XLA Modules:
  0.0 104.6 jit_solution(15847385675903280700)
XLA Ops:
  0.0 6.4 %collective-permute-start.1 = (f32[32,2048]{1,0:T(8,128)}, f32[32,2048]{1,0:T(8,128)S(1)}, u32[]{:S(2)}, u32[]{:S(2)}) collective-permute-start(f32[32,2048]{1,0:T(8,128)} %refs_0_.1), channel_id=1, source_target_pairs={{0,12},{32,51},{4,0},{36,55},{8,4},{40,59},{12,8},{44,63},{16,28},... | collective-permute-start | bytes 786440 | tf_op jit(solution)/shard_map/ppermute | solution.py:45
  6.4 1.0 dynamic-slice_bitcast_fusion.3
  7.5 3.6 %collective-permute-start.19 = (f32[8,4,512]{2,1,0:T(4,128)S(1)}, f32[8,4,512]{2,1,0:T(4,128)S(1)}, u32[]{:S(2)}, u32[]{:S(2)}) collective-permute-start(f32[8,4,512]{2,1,0:T(4,128)S(1)} %get-tuple-element.21), channel_id=1, source_target_pairs={{0,3},{1,0},{2,1},{3,2},{4,7},{5,4},{6,5},{7,6},{8,11},{9,8},{10,9... | collective-permute-start | bytes 196616 | tf_op jit(solution)/shard_map/ppermute | solution.py:207
  11.0 2.8 %collective-permute-start.18 = (f32[8,4,512]{2,1,0:T(4,128)S(1)}, f32[8,4,512]{2,1,0:T(4,128)S(1)}, u32[]{:S(2)}, u32[]{:S(2)}) collective-permute-start(f32[8,4,512]{2,1,0:T(4,128)S(1)} %get-tuple-element.22), channel_id=1, source_target_pairs={{0,2},{1,3},{2,0},{3,1},{4,6},{5,7},{6,4},{7,5},{8,10},{9,11},{10,... | collective-permute-start | bytes 196616 | tf_op jit(solution)/shard_map/ppermute | solution.py:207
  13.8 1.7 %constant_dynamic-update-slice_fusion.3 = f32[128,2048]{1,0:T(8,128)} fusion(f32[32,2048]{1,0:T(8,128)} %refs_0_.1), kind=kLoop, calls=%fused_computation.18 | loop fusion | bytes 524288
  15.5 1.9 %collective-permute-start.3 = (f32[32,2048]{1,0:T(8,128)S(1)}, f32[32,2048]{1,0:T(8,128)S(1)}, u32[]{:S(2)}, u32[]{:S(2)}) collective-permute-start(f32[32,2048]{1,0:T(8,128)S(1)} %collective-permute-done.1.refs_2_), channel_id=1, source_target_pairs={{32,51},{36,55},{40,59},{44,63},{48,32},{52,36},{56,40},{60,44},{3... | collective-permute-start | bytes 786440 | tf_op jit(solution)/shard_map/ppermute | solution.py:45
  17.4 1.5 %collective-permute-start.2 = (f32[32,2048]{1,0:T(8,128)S(1)}, f32[32,2048]{1,0:T(8,128)S(1)}, u32[]{:S(2)}, u32[]{:S(2)}) collective-permute-start(f32[32,2048]{1,0:T(8,128)S(1)} %collective-permute-done.refs_1_), channel_id=1, source_target_pairs={{0,4},{32,48},{4,8},{36,52},{8,12},{40,56},{12,0},{44,60},{16,20},... | collective-permute-start | bytes 786440 | tf_op jit(solution)/shard_map/ppermute | solution.py:45
  19.0 0.7 constant_dynamic-update-slice_fusion.2
  20.4 3.8 %collective-permute-done.2.refs_3_ = f32[32,2048]{1,0:T(8,128)S(1)} collective-permute-done((f32[32,2048]{1,0:T(8,128)S(1)}, f32[32,2048]{1,0:T(8,128)S(1)}, u32[]{:S(2)}, u32[]{:S(2)}) %collective-permute-start.2) | collective-permute-done | bytes 262176 | tf_op jit(solution)/shard_map/ppermute | solution.py:45
  24.2 0.8 constant_dynamic-update-slice_fusion
  25.0 2.4 %collective-permute-start.8 = (f32[128,2048]{1,0:T(8,128)}, f32[128,2048]{1,0:T(8,128)S(1)}, u32[]{:S(2)}, u32[]{:S(2)}) collective-permute-start(f32[128,2048]{1,0:T(8,128)} %constant_dynamic-update-slice_fusion), channel_id=1, source_target_pairs={{0,19},{32,44},{4,23},{36,32},{8,27},{40,36},{12,31},{44,40},{16,0... | collective-permute-start | bytes 3145736 | tf_op jit(solution)/shard_map/ppermute | solution.py:45
  27.4 2.4 %collective-permute-start.4 = (f32[32,2048]{1,0:T(8,128)S(1)}, f32[32,2048]{1,0:T(8,128)S(1)}, u32[]{:S(2)}, u32[]{:S(2)}) collective-permute-start(f32[32,2048]{1,0:T(8,128)S(1)} %collective-permute-done.2.refs_3_), channel_id=1, source_target_pairs={{32,48},{36,52},{40,56},{44,60},{48,33},{52,37},{56,41},{60,45},{3... | collective-permute-start | bytes 786440 | tf_op jit(solution)/shard_map/ppermute | solution.py:45
  30.6 3.6 %collective-permute-start.5 = (f32[32,2048]{1,0:T(8,128)S(1)}, f32[32,2048]{1,0:T(8,128)S(1)}, u32[]{:S(2)}, u32[]{:S(2)}) collective-permute-start(f32[32,2048]{1,0:T(8,128)S(1)} %collective-permute-done.3.refs_4_), channel_id=1, source_target_pairs={{32,51},{36,55},{40,59},{44,63},{48,32},{52,36},{56,40},{60,44},{3... | collective-permute-start | bytes 786440 | tf_op jit(solution)/shard_map/ppermute | solution.py:45
  34.2 4.7 %collective-permute-done.4.refs_5_ = f32[32,2048]{1,0:T(8,128)S(1)} collective-permute-done((f32[32,2048]{1,0:T(8,128)S(1)}, f32[32,2048]{1,0:T(8,128)S(1)}, u32[]{:S(2)}, u32[]{:S(2)}) %collective-permute-start.4) | collective-permute-done | bytes 262176 | tf_op jit(solution)/shard_map/ppermute | solution.py:45
  38.9 1.9 %collective-permute-start.6 = (f32[32,2048]{1,0:T(8,128)S(1)}, f32[32,2048]{1,0:T(8,128)S(1)}, u32[]{:S(2)}, u32[]{:S(2)}) collective-permute-start(f32[32,2048]{1,0:T(8,128)S(1)} %collective-permute-done.4.refs_5_), channel_id=1, source_target_pairs={{32,48},{36,52},{40,56},{44,60},{48,33},{52,37},{56,41},{60,45},{3... | collective-permute-start | bytes 786440 | tf_op jit(solution)/shard_map/ppermute | solution.py:45
  40.9 8.0 %collective-permute-done.6.refs_7_ = f32[32,2048]{1,0:T(8,128)S(1)} collective-permute-done((f32[32,2048]{1,0:T(8,128)S(1)}, f32[32,2048]{1,0:T(8,128)S(1)}, u32[]{:S(2)}, u32[]{:S(2)}) %collective-permute-start.6) | collective-permute-done | bytes 262176 | tf_op jit(solution)/shard_map/ppermute | solution.py:45
  49.8 1.8 %collective-permute-start.10 = (f32[128,2048]{1,0:T(8,128)S(1)}, f32[128,2048]{1,0:T(8,128)S(1)}, u32[]{:S(2)}, u32[]{:S(2)}) collective-permute-start(f32[128,2048]{1,0:T(8,128)S(1)} %get-tuple-element.15), channel_id=1, source_target_pairs={{0,19},{32,44},{4,23},{36,32},{8,27},{40,36},{12,31},{44,40},{16,0... | collective-permute-start | bytes 3145736 | tf_op jit(solution)/shard_map/ppermute | solution.py:45
  51.9 2.6 %collective-permute-start.21 = (f32[4,8,8,512]{3,2,1,0:T(8,128)S(1)}, f32[4,8,8,512]{3,2,1,0:T(8,128)S(1)}, u32[]{:S(2)}, u32[]{:S(2)}) collective-permute-start(f32[4,8,8,512]{3,2,1,0:T(8,128)S(1)} %pad_maximum_fusion.own), channel_id=1, source_target_pairs={{0,64},{32,224},{64,128},{96,32},{128,192},{160,96},{192,0},{224,1... | collective-permute-start | bytes 1572872 | tf_op jit(solution)/shard_map/ppermute | solution.py:27
  54.5 6.1 %collective-permute-done.21.near = f32[4,8,8,512]{3,2,1,0:T(8,128)S(1)} collective-permute-done((f32[4,8,8,512]{3,2,1,0:T(8,128)S(1)}, f32[4,8,8,512]{3,2,1,0:T(8,128)S(1)}, u32[]{:S(2)}, u32[]{:S(2)}) %collective-permute-start.21) | collective-permute-done | bytes 524320 | tf_op jit(solution)/shard_map/ppermute | solution.py:27
  60.6 3.5 %collective-permute-start.23 = (f32[2,8,8,512]{3,2,1,0:T(8,128)S(1)}, f32[2,8,8,512]{3,2,1,0:T(8,128)S(1)}, u32[]{:S(2)}, u32[]{:S(2)}) collective-permute-start(f32[2,8,8,512]{3,2,1,0:T(8,128)S(1)} %slice_select_fusion.3), channel_id=1, source_target_pairs={{0,64},{32,224},{64,128},{96,32},{128,192},{160,96},{192,0},{224,1... | collective-permute-start | bytes 786440 | tf_op jit(solution)/shard_map/ppermute | solution.py:27
  64.1 1.2 %fusion = (f32[64,2048]{1,0:T(8,128)}, f32[64,2048]{1,0:T(8,128)}) fusion(f32[128,2048]{1,0:T(8,128)S(1)} %collective-permute-done.10.refs_11_, f32[128,2048]{1,0:T(8,128)S(1)} %collective-permute-done.8.refs_9_, pred[]{:T(512)S(6)} %eq.392), kind=kLoop, calls=%fused_computation.27 | loop fusion | flops 131072 | bytes 2621441 | tf_op jit(solution)/shard_map/slice | solution.py:219
  65.3 2.6 %collective-permute-start.14 = (f32[64,2048]{1,0:T(8,128)}, f32[64,2048]{1,0:T(8,128)}, u32[]{:S(2)}, u32[]{:S(2)}) collective-permute-start(f32[64,2048]{1,0:T(8,128)} %get-tuple-element.11), channel_id=1, source_target_pairs={{0,19},{32,44},{4,23},{36,32},{8,27},{40,36},{12,31},{44,40},{16,0... | collective-permute-start | bytes 1572872 | tf_op jit(solution)/shard_map/ppermute | solution.py:45
  68.0 1.3 %collective-permute-done.9.refs_10_ = f32[128,2048]{1,0:T(8,128)S(1)} collective-permute-done((f32[128,2048]{1,0:T(8,128)S(1)}, f32[128,2048]{1,0:T(8,128)S(1)}, u32[]{:S(2)}, u32[]{:S(2)}) %collective-permute-start.9) | collective-permute-done | bytes 1048608 | tf_op jit(solution)/shard_map/ppermute | solution.py:45
  69.3 1.0 slice_select_fusion.1
  71.2 2.6 %collective-permute-start.13 = (f32[64,2048]{1,0:T(8,128)}, f32[64,2048]{1,0:T(8,128)}, u32[]{:S(2)}, u32[]{:S(2)}) collective-permute-start(f32[64,2048]{1,0:T(8,128)} %get-tuple-element.12), channel_id=1, source_target_pairs={{0,19},{32,44},{4,23},{36,32},{8,27},{40,36},{12,31},{44,40},{16,0... | collective-permute-start | bytes 1572872 | tf_op jit(solution)/shard_map/ppermute | solution.py:45
  74.4 1.5 %collective-permute-start.16 = (f32[64,2048]{1,0:T(8,128)}, f32[64,2048]{1,0:T(8,128)}, u32[]{:S(2)}, u32[]{:S(2)}) collective-permute-start(f32[64,2048]{1,0:T(8,128)} %collective-permute-done.14.refs_15_), channel_id=1, source_target_pairs={{0,19},{4,23},{8,27},{12,31},{16,0},{20,4},{24,8},{28,12},{1,16},{... | collective-permute-start | bytes 1572872 | tf_op jit(solution)/shard_map/ppermute | solution.py:45
  75.9 4.4 %collective-permute-done.11.refs_12_ = f32[64,2048]{1,0:T(8,128)S(1)} collective-permute-done((f32[64,2048]{1,0:T(8,128)}, f32[64,2048]{1,0:T(8,128)S(1)}, u32[]{:S(2)}, u32[]{:S(2)}) %collective-permute-start.11) | collective-permute-done | bytes 524320 | tf_op jit(solution)/shard_map/ppermute | solution.py:45
  80.3 1.5 %collective-permute-start.15 = (f32[64,2048]{1,0:T(8,128)S(1)}, f32[64,2048]{1,0:T(8,128)}, u32[]{:S(2)}, u32[]{:S(2)}) collective-permute-start(f32[64,2048]{1,0:T(8,128)S(1)} %collective-permute-done.11.refs_12_), channel_id=1, source_target_pairs={{0,16},{4,20},{8,24},{12,28},{16,1},{20,5},{24,9},{28,13},{1,17},{... | collective-permute-start | bytes 1572872 | tf_op jit(solution)/shard_map/ppermute | solution.py:45
  83.3 0.8 stack.315.runs
  85.4 0.8 copy-done.6
  86.2 4.1 %shard_map.55 = (bf16[1024,512]{1,0:T(8,128)(2,1)}, bf16[1024,512]{1,0:T(8,128)(2,1)}) custom-call(s32[3]{0:T(128)} %pad_add_fusion.place, f32[4,8,8,512]{3,2,1,0:T(8,128)} %copy-done.2, f32[4,8,8,512]{3,2,1,0:T(8,128)} %copy-done.3, f32[4,8,8,512]{3,2,1,0:T(8,128)} %copy-done.6, f32[2,8,8,512]{3,2,1,0:T(8,128)} %copy-done.7, f32[2,8,8,512]{3,2,1,0:T(8,128)} %copy-done.8, ...), custom_call_target="tpu_custom_call" | custom-call | tf_op jit(solution)/shard_map/pallas_call | solution.py:79
  90.4 14.0 %shard_map.56 = f32[2048,512]{1,0:T(8,128)} custom-call(s32[72]{0:T(128)} %stack.315.runs, f32[32,2048]{1,0:T(8,128)} %refs_0_.1, f32[32,2048]{1,0:T(8,128)} %copy-done.10, f32[32,2048]{1,0:T(8,128)} %copy-done.9, f32[32,2048]{1,0:T(8,128)} %copy-done.12, f32[32,2048]{1,0:T(8,128)} %copy-done.11, f32[32,2048]{1,0:T(8,128)} %copy-done.13, ...), custom_call_target="tpu_custom_call" | custom-call | flops 6442450944 | bytes 19922944 | tf_op jit(solution)/shard_map/pallas_call | solution.py:166
  (83 shorter events, 6.4 us)
Async XLA Ops:
  0.0 15.5 %collective-permute-start.1 = (f32[32,2048]{1,0:T(8,128)}, f32[32,2048]{1,0:T(8,128)S(1)}, u32[]{:S(2)}, u32[]{:S(2)}) collective-permute-start(f32[32,2048]{1,0:T(8,128)} %refs_0_.1), channel_id=1, source_target_pairs={{0,12},{32,51},{4,0},{36,55},{8,4},{40,59},{12,8},{44,63},{16,28},... | collective-permute-start | bytes 786440 | tf_op jit(solution)/shard_map/ppermute | solution.py:45
  6.4 11.0 %collective-permute-start = (f32[32,2048]{1,0:T(8,128)}, f32[32,2048]{1,0:T(8,128)S(1)}, u32[]{:S(2)}, u32[]{:S(2)}) collective-permute-start(f32[32,2048]{1,0:T(8,128)} %refs_0_.1), channel_id=1, source_target_pairs={{0,4},{32,48},{4,8},{36,52},{8,12},{40,56},{12,0},{44,60},{16,20},... | collective-permute-start | bytes 786440 | tf_op jit(solution)/shard_map/ppermute | solution.py:45
  7.4 20.1 %collective-permute-start.17 = (f32[8,4,512]{2,1,0:T(4,128)S(1)}, f32[8,4,512]{2,1,0:T(4,128)S(1)}, u32[]{:S(2)}, u32[]{:S(2)}) collective-permute-start(f32[8,4,512]{2,1,0:T(4,128)S(1)} %get-tuple-element.20), channel_id=1, source_target_pairs={{0,1},{1,2},{2,3},{3,0},{4,5},{5,6},{6,7},{7,4},{8,9},{9,10},{10,1... | collective-permute-start | bytes 196616 | tf_op jit(solution)/shard_map/ppermute | solution.py:207
  7.5 20.0 %collective-permute-start.19 = (f32[8,4,512]{2,1,0:T(4,128)S(1)}, f32[8,4,512]{2,1,0:T(4,128)S(1)}, u32[]{:S(2)}, u32[]{:S(2)}) collective-permute-start(f32[8,4,512]{2,1,0:T(4,128)S(1)} %get-tuple-element.21), channel_id=1, source_target_pairs={{0,3},{1,0},{2,1},{3,2},{4,7},{5,4},{6,5},{7,6},{8,11},{9,8},{10,9... | collective-permute-start | bytes 196616 | tf_op jit(solution)/shard_map/ppermute | solution.py:207
  11.0 18.9 %collective-permute-start.18 = (f32[8,4,512]{2,1,0:T(4,128)S(1)}, f32[8,4,512]{2,1,0:T(4,128)S(1)}, u32[]{:S(2)}, u32[]{:S(2)}) collective-permute-start(f32[8,4,512]{2,1,0:T(4,128)S(1)} %get-tuple-element.22), channel_id=1, source_target_pairs={{0,2},{1,3},{2,0},{3,1},{4,6},{5,7},{6,4},{7,5},{8,10},{9,11},{10,... | collective-permute-start | bytes 196616 | tf_op jit(solution)/shard_map/ppermute | solution.py:207
  15.5 34.3 %copy-start.9 = (f32[32,2048]{1,0:T(8,128)}, f32[32,2048]{1,0:T(8,128)S(1)}, u32[]{:S(2)}) copy-start(f32[32,2048]{1,0:T(8,128)S(1)} %collective-permute-done.1.refs_2_) | copy-start | bytes 786436
  15.5 15.1 %collective-permute-start.3 = (f32[32,2048]{1,0:T(8,128)S(1)}, f32[32,2048]{1,0:T(8,128)S(1)}, u32[]{:S(2)}, u32[]{:S(2)}) collective-permute-start(f32[32,2048]{1,0:T(8,128)S(1)} %collective-permute-done.1.refs_2_), channel_id=1, source_target_pairs={{32,51},{36,55},{40,59},{44,63},{48,32},{52,36},{56,40},{60,44},{3... | collective-permute-start | bytes 786440 | tf_op jit(solution)/shard_map/ppermute | solution.py:45
  17.4 6.8 %collective-permute-start.2 = (f32[32,2048]{1,0:T(8,128)S(1)}, f32[32,2048]{1,0:T(8,128)S(1)}, u32[]{:S(2)}, u32[]{:S(2)}) collective-permute-start(f32[32,2048]{1,0:T(8,128)S(1)} %collective-permute-done.refs_1_), channel_id=1, source_target_pairs={{0,4},{32,48},{4,8},{36,52},{8,12},{40,56},{12,0},{44,60},{16,20},... | collective-permute-start | bytes 786440 | tf_op jit(solution)/shard_map/ppermute | solution.py:45
  24.2 25.5 %copy-start.12 = (f32[32,2048]{1,0:T(8,128)}, f32[32,2048]{1,0:T(8,128)S(1)}, u32[]{:S(2)}) copy-start(f32[32,2048]{1,0:T(8,128)S(1)} %collective-permute-done.2.refs_3_) | copy-start | bytes 786436
  25.0 23.9 %collective-permute-start.8 = (f32[128,2048]{1,0:T(8,128)}, f32[128,2048]{1,0:T(8,128)S(1)}, u32[]{:S(2)}, u32[]{:S(2)}) collective-permute-start(f32[128,2048]{1,0:T(8,128)} %constant_dynamic-update-slice_fusion), channel_id=1, source_target_pairs={{0,19},{32,44},{4,23},{36,32},{8,27},{40,36},{12,31},{44,40},{16,0... | collective-permute-start | bytes 3145736 | tf_op jit(solution)/shard_map/ppermute | solution.py:45
  27.4 22.1 %collective-permute-start.7 = (f32[128,2048]{1,0:T(8,128)}, f32[128,2048]{1,0:T(8,128)S(1)}, u32[]{:S(2)}, u32[]{:S(2)}) collective-permute-start(f32[128,2048]{1,0:T(8,128)} %constant_dynamic-update-slice_fusion), channel_id=1, source_target_pairs={{0,16},{32,36},{4,20},{36,40},{8,24},{40,44},{12,28},{44,32},{16,1... | collective-permute-start | bytes 3145736 | tf_op jit(solution)/shard_map/ppermute | solution.py:45
  27.4 11.4 %collective-permute-start.4 = (f32[32,2048]{1,0:T(8,128)S(1)}, f32[32,2048]{1,0:T(8,128)S(1)}, u32[]{:S(2)}, u32[]{:S(2)}) collective-permute-start(f32[32,2048]{1,0:T(8,128)S(1)} %collective-permute-done.2.refs_3_), channel_id=1, source_target_pairs={{32,48},{36,52},{40,56},{44,60},{48,33},{52,37},{56,41},{60,45},{3... | collective-permute-start | bytes 786440 | tf_op jit(solution)/shard_map/ppermute | solution.py:45
  30.0 21.6 %collective-permute-start.20 = (f32[4,8,4,512]{3,2,1,0:T(4,128)S(1)}, f32[4,8,4,512]{3,2,1,0:T(4,128)S(1)}, u32[]{:S(2)}, u32[]{:S(2)}) collective-permute-start(f32[4,8,4,512]{3,2,1,0:T(4,128)S(1)} %pad_maximum_fusion.1), channel_id=1, source_target_pairs={{0,32},{32,0},{1,33},{33,1},{2,34},{34,2},{3,35},{35,3},{4,36},{36... | collective-permute-start | bytes 786440 | tf_op jit(solution)/shard_map/ppermute | solution.py:31
  30.6 21.2 %copy-start.11 = (f32[32,2048]{1,0:T(8,128)}, f32[32,2048]{1,0:T(8,128)S(1)}, u32[]{:S(2)}) copy-start(f32[32,2048]{1,0:T(8,128)S(1)} %collective-permute-done.3.refs_4_) | copy-start | bytes 786436
  30.6 10.3 %collective-permute-start.5 = (f32[32,2048]{1,0:T(8,128)S(1)}, f32[32,2048]{1,0:T(8,128)S(1)}, u32[]{:S(2)}, u32[]{:S(2)}) collective-permute-start(f32[32,2048]{1,0:T(8,128)S(1)} %collective-permute-done.3.refs_4_), channel_id=1, source_target_pairs={{32,51},{36,55},{40,59},{44,63},{48,32},{52,36},{56,40},{60,44},{3... | collective-permute-start | bytes 786440 | tf_op jit(solution)/shard_map/ppermute | solution.py:45
  38.9 10.0 %collective-permute-start.6 = (f32[32,2048]{1,0:T(8,128)S(1)}, f32[32,2048]{1,0:T(8,128)S(1)}, u32[]{:S(2)}, u32[]{:S(2)}) collective-permute-start(f32[32,2048]{1,0:T(8,128)S(1)} %collective-permute-done.4.refs_5_), channel_id=1, source_target_pairs={{32,48},{36,52},{40,56},{44,60},{48,33},{52,37},{56,41},{60,45},{3... | collective-permute-start | bytes 786440 | tf_op jit(solution)/shard_map/ppermute | solution.py:45
  49.8 20.8 %copy-start.16 = (s32[8,128]{1,0:T(8,128)S(1)}, s32[8,128]{1,0:T(8,128)}, u32[]{:S(2)}) copy-start(s32[8,128]{1,0:T(8,128)} %param.7) | copy-start | bytes 12292
  49.8 14.3 %collective-permute-start.10 = (f32[128,2048]{1,0:T(8,128)S(1)}, f32[128,2048]{1,0:T(8,128)S(1)}, u32[]{:S(2)}, u32[]{:S(2)}) collective-permute-start(f32[128,2048]{1,0:T(8,128)S(1)} %get-tuple-element.15), channel_id=1, source_target_pairs={{0,19},{32,44},{4,23},{36,32},{8,27},{40,36},{12,31},{44,40},{16,0... | collective-permute-start | bytes 3145736 | tf_op jit(solution)/shard_map/ppermute | solution.py:45
  51.8 30.7 %copy-start.17 = (s32[8,128]{1,0:T(8,128)S(1)}, s32[8,128]{1,0:T(8,128)}, u32[]{:S(2)}) copy-start(s32[8,128]{1,0:T(8,128)} %param.8) | copy-start | bytes 12292
  51.9 33.5 %copy-start.2 = (f32[4,8,8,512]{3,2,1,0:T(8,128)}, f32[4,8,8,512]{3,2,1,0:T(8,128)S(1)}, u32[]{:S(2)}) copy-start(f32[4,8,8,512]{3,2,1,0:T(8,128)S(1)} %pad_maximum_fusion.own) | copy-start | bytes 1572868
  51.9 8.7 %collective-permute-start.21 = (f32[4,8,8,512]{3,2,1,0:T(8,128)S(1)}, f32[4,8,8,512]{3,2,1,0:T(8,128)S(1)}, u32[]{:S(2)}, u32[]{:S(2)}) collective-permute-start(f32[4,8,8,512]{3,2,1,0:T(8,128)S(1)} %pad_maximum_fusion.own), channel_id=1, source_target_pairs={{0,64},{32,224},{64,128},{96,32},{128,192},{160,96},{192,0},{224,1... | collective-permute-start | bytes 1572872 | tf_op jit(solution)/shard_map/ppermute | solution.py:27
  54.5 14.9 %collective-permute-start.9 = (f32[128,2048]{1,0:T(8,128)S(1)}, f32[128,2048]{1,0:T(8,128)S(1)}, u32[]{:S(2)}, u32[]{:S(2)}) collective-permute-start(f32[128,2048]{1,0:T(8,128)S(1)} %get-tuple-element.16), channel_id=1, source_target_pairs={{0,16},{32,36},{4,20},{36,40},{8,24},{40,44},{12,28},{44,32},{16,1... | collective-permute-start | bytes 3145736 | tf_op jit(solution)/shard_map/ppermute | solution.py:45
  60.6 24.8 %copy-start.3 = (f32[4,8,8,512]{3,2,1,0:T(8,128)}, f32[4,8,8,512]{3,2,1,0:T(8,128)S(1)}, u32[]{:S(2)}) copy-start(f32[4,8,8,512]{3,2,1,0:T(8,128)S(1)} %collective-permute-done.21.near) | copy-start | bytes 1572868
  60.6 9.9 %collective-permute-start.23 = (f32[2,8,8,512]{3,2,1,0:T(8,128)S(1)}, f32[2,8,8,512]{3,2,1,0:T(8,128)S(1)}, u32[]{:S(2)}, u32[]{:S(2)}) collective-permute-start(f32[2,8,8,512]{3,2,1,0:T(8,128)S(1)} %slice_select_fusion.3), channel_id=1, source_target_pairs={{0,64},{32,224},{64,128},{96,32},{128,192},{160,96},{192,0},{224,1... | collective-permute-start | bytes 786440 | tf_op jit(solution)/shard_map/ppermute | solution.py:27
  65.3 9.1 %collective-permute-start.14 = (f32[64,2048]{1,0:T(8,128)}, f32[64,2048]{1,0:T(8,128)}, u32[]{:S(2)}, u32[]{:S(2)}) collective-permute-start(f32[64,2048]{1,0:T(8,128)} %get-tuple-element.11), channel_id=1, source_target_pairs={{0,19},{32,44},{4,23},{36,32},{8,27},{40,36},{12,31},{44,40},{16,0... | collective-permute-start | bytes 1572872 | tf_op jit(solution)/shard_map/ppermute | solution.py:45
  70.5 9.9 %collective-permute-start.11 = (f32[64,2048]{1,0:T(8,128)}, f32[64,2048]{1,0:T(8,128)S(1)}, u32[]{:S(2)}, u32[]{:S(2)}) collective-permute-start(f32[64,2048]{1,0:T(8,128)} %get-tuple-element.14), channel_id=1, source_target_pairs={{0,16},{32,36},{4,20},{36,40},{8,24},{40,44},{12,28},{44,32},{16,1... | collective-permute-start | bytes 1572872 | tf_op jit(solution)/shard_map/ppermute | solution.py:45
  70.5 3.3 %collective-permute-start.24 = (f32[2,8,8,512]{3,2,1,0:T(8,128)S(1)}, f32[2,8,8,512]{3,2,1,0:T(8,128)S(1)}, u32[]{:S(2)}, u32[]{:S(2)}) collective-permute-start(f32[2,8,8,512]{3,2,1,0:T(8,128)S(1)} %collective-permute-done.23.far), channel_id=1, source_target_pairs={{0,32},{32,0},{1,33},{33,1},{2,34},{34,2},{3,35},{35,3},{4,36},{36... | collective-permute-start | bytes 786440 | tf_op jit(solution)/shard_map/ppermute | solution.py:31
  70.8 14.6 %collective-permute-start.22 = (f32[4,8,8,512]{3,2,1,0:T(8,128)S(1)}, f32[4,8,8,512]{3,2,1,0:T(8,128)S(1)}, u32[]{:S(2)}, u32[]{:S(2)}) collective-permute-start(f32[4,8,8,512]{3,2,1,0:T(8,128)S(1)} %collective-permute-done.21.near), channel_id=1, source_target_pairs={{0,32},{32,0},{1,33},{33,1},{2,34},{34,2},{3,35},{35,3},{4,36},{36... | collective-permute-start | bytes 1572872 | tf_op jit(solution)/shard_map/ppermute | solution.py:31
  71.2 19.1 %collective-permute-start.13 = (f32[64,2048]{1,0:T(8,128)}, f32[64,2048]{1,0:T(8,128)}, u32[]{:S(2)}, u32[]{:S(2)}) collective-permute-start(f32[64,2048]{1,0:T(8,128)} %get-tuple-element.12), channel_id=1, source_target_pairs={{0,19},{32,44},{4,23},{36,32},{8,27},{40,36},{12,31},{44,40},{16,0... | collective-permute-start | bytes 1572872 | tf_op jit(solution)/shard_map/ppermute | solution.py:45
  73.8 16.5 %collective-permute-start.12 = (f32[64,2048]{1,0:T(8,128)S(1)}, f32[64,2048]{1,0:T(8,128)}, u32[]{:S(2)}, u32[]{:S(2)}) collective-permute-start(f32[64,2048]{1,0:T(8,128)S(1)} %get-tuple-element.13), channel_id=1, source_target_pairs={{0,16},{32,36},{4,20},{36,40},{8,24},{40,44},{12,28},{44,32},{16,1... | collective-permute-start | bytes 1572872 | tf_op jit(solution)/shard_map/ppermute | solution.py:45
  74.4 15.9 %collective-permute-start.16 = (f32[64,2048]{1,0:T(8,128)}, f32[64,2048]{1,0:T(8,128)}, u32[]{:S(2)}, u32[]{:S(2)}) collective-permute-start(f32[64,2048]{1,0:T(8,128)} %collective-permute-done.14.refs_15_), channel_id=1, source_target_pairs={{0,19},{4,23},{8,27},{12,31},{16,0},{20,4},{24,8},{28,12},{1,16},{... | collective-permute-start | bytes 1572872 | tf_op jit(solution)/shard_map/ppermute | solution.py:45
  80.3 10.0 %collective-permute-start.15 = (f32[64,2048]{1,0:T(8,128)S(1)}, f32[64,2048]{1,0:T(8,128)}, u32[]{:S(2)}, u32[]{:S(2)}) collective-permute-start(f32[64,2048]{1,0:T(8,128)S(1)} %collective-permute-done.11.refs_12_), channel_id=1, source_target_pairs={{0,16},{4,20},{8,24},{12,28},{16,1},{20,5},{24,9},{28,13},{1,17},{... | collective-permute-start | bytes 1572872 | tf_op jit(solution)/shard_map/ppermute | solution.py:45
  (12 other events, 105.8 us)

commit v4 on v2

--- a/solution.py
+++ b/solution.py
@@ -196,8 +196,10 @@
     s1u, s1d = cross(left, 1), cross(left, -1)
     s2u, s2d = cross(s1u, 1), cross(s1d, -1, (1,))
 
-    m1 = join(left, s1u, s1d, s2u)
-    u1, d1 = cross(m1, 1, flip=True), cross(m1, -1, flip=True)
+    m1 = join(left, s1u, s1d)
+    u1a, d1a = cross(m1, 1, flip=True), cross(m1, -1, flip=True)
+    u1b, d1b = cross(s2u, 1, flip=True), cross(s2u, -1, flip=True)
+    u1, d1 = join(u1a, u1b), join(d1a, d1b)
     s3u, s3d = cross(s2u, 1, (1,)), cross(s2d, -1, (1,))
     s4 = cross(s3u, 1, (1,))
 
@@ -275,8 +277,8 @@
     mask = jnp.pad(jnp.repeat(left_tiles, KT, axis=1), ((0, 8), (0, 0)))
 
     u4, d4 = cross(u3a, 1, (0,), True), cross(d3b, -1, (0,), True)
-    hi, lo = assemble_right(after(place, u1, d1), [both, near, near_o, far, far_o], right_mask)
-    pieces = [left, s1u, s1d, s2u, s2d, s3u, s3d, s4, u1, d1, u2, d2, u3a, u3b, d3a, d3b, u4, d4]
+    hi, lo = assemble_right(after(place, u1a, d1a), [both, near, near_o, far, far_o], right_mask)
+    pieces = [left, s1u, s1d, s2u, s2d, s3u, s3d, s4, u1a, u1b, d1a, d1b, u2, d2, u3a, u3b, d3a, d3b, u4, d4]
     return product(runs, pieces, mask, hi, lo, accum)
 
 

time: 105 us -> 104 us (level)
  starting transfers between devices: 43.9 us -> 50 us
  waiting for transfers between devices: 29 us -> 24.8 us
  local copies, waits for them, and re-layouts: 8.93 us -> 6.03 us
    ppermute x17 -> x19, starting transfers between devices: 30.2 us -> 35.5 us  [cross(): return lax.ppermute(a, ('core', 'zlo', 'y', 'zhi'), pairs)]
    ppermute x17 -> x19, waiting for transfers between devices: 22.9 us -> 18.6 us  [cross(): return lax.ppermute(a, ('core', 'zlo', 'y', 'zhi'), pairs)]
    unnamed x44, local copies, waits for them, and re-layouts: 4.83 us -> 2.72 us
  transfers between devices with their start and end apart: 25 -> 27, of which waited for: 7 -> 7; matrix products, arithmetic and copies ran while one was open for 10% -> 8% of each run, Pallas kernels for 4% -> 4%
where the time goes in v4:
time: 104 us
  starting transfers between devices  50 us (48%)
  waiting for transfers between devices  24.8 us (24%)
  Pallas kernels  18.5 us (18%)
  local copies, waits for them, and re-layouts  6.03 us (6%)
  other arithmetic  3.57 us (3%)
  between operations  1.23 us (1%)
    ppermute x19, starting transfers between devices, cross(): return lax.ppermute(a, ('core', 'zlo', 'y', 'zhi'), pairs)  35.5 us
    ppermute x19, waiting for transfers between devices, cross(): return lax.ppermute(a, ('core', 'zlo', 'y', 'zhi'), pairs)  18.6 us
    pallas_call x1, Pallas kernels, product(): pl.pallas_call(functools.partial(product_kernel, heights), out_shape=jax....  14.4 us
    ppermute x3, starting transfers between devices, body(): layers.append(part if s == 0 else lax.ppermute(part, 'zhi', ring(4, s)))  6.44 us
    ppermute x2, starting transfers between devices, along_x(): return lax.ppermute(a, ('x', 'core'), pairs)  6.22 us
    ppermute x2, waiting for transfers between devices, along_x(): return lax.ppermute(a, ('x', 'core'), pairs)  6.13 us
    pallas_call x1, Pallas kernels, assemble_right(): pl.pallas_call(right_kernel, out_shape=[jax.ShapeDtypeStruct((1024, 512),...  4.1 us
    unnamed x44, local copies, waits for them, and re-layouts  2.72 us
  transfers between devices with their start and end apart: 27, of which 7 were waited for; matrix products, arithmetic and copies ran while one was open for 8% of the time, Pallas kernels for 4%

profile of v4, /device:TPU:1, one launch (start us, length us, event | category | flops | bytes accessed | tf_op | source)
XLA Modules:
  0.0 104.1 jit_solution(8758403677689662155)
XLA Ops:
  0.0 6.4 %collective-permute-start.1 = (f32[32,2048]{1,0:T(8,128)}, f32[32,2048]{1,0:T(8,128)S(1)}, u32[]{:S(2)}, u32[]{:S(2)}) collective-permute-start(f32[32,2048]{1,0:T(8,128)} %refs_0_.1), channel_id=1, source_target_pairs={{0,12},{32,51},{4,0},{36,55},{8,4},{40,59},{12,8},{44,63},{16,28},... | collective-permute-start | bytes 786440 | tf_op jit(solution)/shard_map/ppermute | solution.py:45
  6.4 1.0 dynamic-slice_bitcast_fusion.3
  7.5 3.6 %collective-permute-start.21 = (f32[8,4,512]{2,1,0:T(4,128)S(1)}, f32[8,4,512]{2,1,0:T(4,128)S(1)}, u32[]{:S(2)}, u32[]{:S(2)}) collective-permute-start(f32[8,4,512]{2,1,0:T(4,128)S(1)} %get-tuple-element.21), channel_id=1, source_target_pairs={{0,3},{1,0},{2,1},{3,2},{4,7},{5,4},{6,5},{7,6},{8,11},{9,8},{10,9... | collective-permute-start | bytes 196616 | tf_op jit(solution)/shard_map/ppermute | solution.py:210
  11.0 2.8 %collective-permute-start.20 = (f32[8,4,512]{2,1,0:T(4,128)S(1)}, f32[8,4,512]{2,1,0:T(4,128)S(1)}, u32[]{:S(2)}, u32[]{:S(2)}) collective-permute-start(f32[8,4,512]{2,1,0:T(4,128)S(1)} %get-tuple-element.22), channel_id=1, source_target_pairs={{0,2},{1,3},{2,0},{3,1},{4,6},{5,7},{6,4},{7,5},{8,10},{9,11},{10,... | collective-permute-start | bytes 196616 | tf_op jit(solution)/shard_map/ppermute | solution.py:210
  13.8 1.0 constant_dynamic-update-slice_fusion.2
  14.8 1.9 %collective-permute-start.3 = (f32[32,2048]{1,0:T(8,128)S(1)}, f32[32,2048]{1,0:T(8,128)S(1)}, u32[]{:S(2)}, u32[]{:S(2)}) collective-permute-start(f32[32,2048]{1,0:T(8,128)S(1)} %collective-permute-done.1.refs_2_), channel_id=1, source_target_pairs={{32,51},{36,55},{40,59},{44,63},{48,32},{52,36},{56,40},{60,44},{3... | collective-permute-start | bytes 786440 | tf_op jit(solution)/shard_map/ppermute | solution.py:45
  16.8 1.5 %collective-permute-start.2 = (f32[32,2048]{1,0:T(8,128)S(1)}, f32[32,2048]{1,0:T(8,128)S(1)}, u32[]{:S(2)}, u32[]{:S(2)}) collective-permute-start(f32[32,2048]{1,0:T(8,128)S(1)} %collective-permute-done.refs_1_), channel_id=1, source_target_pairs={{0,4},{32,48},{4,8},{36,52},{8,12},{40,56},{12,0},{44,60},{16,20},... | collective-permute-start | bytes 786440 | tf_op jit(solution)/shard_map/ppermute | solution.py:45
  18.3 2.8 %collective-permute-start.9 = (f32[96,2048]{1,0:T(8,128)S(1)}, f32[96,2048]{1,0:T(8,128)S(1)}, u32[]{:S(2)}, u32[]{:S(2)}) collective-permute-start(f32[96,2048]{1,0:T(8,128)S(1)} %constant_dynamic-update-slice_fusion), channel_id=1, source_target_pairs={{0,19},{32,44},{4,23},{36,32},{8,27},{40,36},{12,31},{44,40},{16,0... | collective-permute-start | bytes 2359304 | tf_op jit(solution)/shard_map/ppermute | solution.py:45
  21.2 2.4 %collective-permute-done.2.refs_3_ = f32[32,2048]{1,0:T(8,128)S(1)} collective-permute-done((f32[32,2048]{1,0:T(8,128)S(1)}, f32[32,2048]{1,0:T(8,128)S(1)}, u32[]{:S(2)}, u32[]{:S(2)}) %collective-permute-start.2) | collective-permute-done | bytes 262176 | tf_op jit(solution)/shard_map/ppermute | solution.py:45
  23.6 2.1 %collective-permute-start.4 = (f32[32,2048]{1,0:T(8,128)S(1)}, f32[32,2048]{1,0:T(8,128)S(1)}, u32[]{:S(2)}, u32[]{:S(2)}) collective-permute-start(f32[32,2048]{1,0:T(8,128)S(1)} %collective-permute-done.2.refs_3_), channel_id=1, source_target_pairs={{32,48},{36,52},{40,56},{44,60},{48,33},{52,37},{56,41},{60,45},{3... | collective-permute-start | bytes 786440 | tf_op jit(solution)/shard_map/ppermute | solution.py:45
  25.8 1.3 %collective-permute-start.22 = (f32[4,8,4,512]{3,2,1,0:T(4,128)S(1)}, f32[4,8,4,512]{3,2,1,0:T(4,128)S(1)}, u32[]{:S(2)}, u32[]{:S(2)}) collective-permute-start(f32[4,8,4,512]{3,2,1,0:T(4,128)S(1)} %pad_maximum_fusion.1), channel_id=1, source_target_pairs={{0,32},{32,0},{1,33},{33,1},{2,34},{34,2},{3,35},{35,3},{4,36},{36... | collective-permute-start | bytes 786440 | tf_op jit(solution)/shard_map/ppermute | solution.py:31
  27.3 4.0 %collective-permute-start.5 = (f32[32,2048]{1,0:T(8,128)S(1)}, f32[32,2048]{1,0:T(8,128)S(1)}, u32[]{:S(2)}, u32[]{:S(2)}) collective-permute-start(f32[32,2048]{1,0:T(8,128)S(1)} %collective-permute-done.3.refs_4_), channel_id=1, source_target_pairs={{32,51},{36,55},{40,59},{44,63},{48,32},{52,36},{56,40},{60,44},{3... | collective-permute-start | bytes 786440 | tf_op jit(solution)/shard_map/ppermute | solution.py:45
  31.4 1.4 %collective-permute-done.4.refs_5_ = f32[32,2048]{1,0:T(8,128)S(1)} collective-permute-done((f32[32,2048]{1,0:T(8,128)S(1)}, f32[32,2048]{1,0:T(8,128)S(1)}, u32[]{:S(2)}, u32[]{:S(2)}) %collective-permute-start.4) | collective-permute-done | bytes 262176 | tf_op jit(solution)/shard_map/ppermute | solution.py:45
  32.7 2.8 %collective-permute-start.10 = (f32[32,2048]{1,0:T(8,128)S(1)}, f32[32,2048]{1,0:T(8,128)S(1)}, u32[]{:S(2)}, u32[]{:S(2)}) collective-permute-start(f32[32,2048]{1,0:T(8,128)S(1)} %collective-permute-done.2.refs_3_), channel_id=1, source_target_pairs={{0,19},{32,44},{4,23},{36,32},{8,27},{40,36},{12,31},{44,40},{16,0... | collective-permute-start | bytes 786440 | tf_op jit(solution)/shard_map/ppermute | solution.py:45
  35.6 1.8 %collective-permute-done.5.refs_6_ = f32[32,2048]{1,0:T(8,128)S(1)} collective-permute-done((f32[32,2048]{1,0:T(8,128)S(1)}, f32[32,2048]{1,0:T(8,128)S(1)}, u32[]{:S(2)}, u32[]{:S(2)}) %collective-permute-start.5) | collective-permute-done | bytes 262176 | tf_op jit(solution)/shard_map/ppermute | solution.py:45
  37.3 1.0 collective-permute-start.8
  38.4 2.5 %collective-permute-start.6 = (f32[32,2048]{1,0:T(8,128)S(1)}, f32[32,2048]{1,0:T(8,128)S(1)}, u32[]{:S(2)}, u32[]{:S(2)}) collective-permute-start(f32[32,2048]{1,0:T(8,128)S(1)} %collective-permute-done.4.refs_5_), channel_id=1, source_target_pairs={{32,48},{36,52},{40,56},{44,60},{48,33},{52,37},{56,41},{60,45},{3... | collective-permute-start | bytes 786440 | tf_op jit(solution)/shard_map/ppermute | solution.py:45
  41.0 5.9 %collective-permute-done.6.refs_7_ = f32[32,2048]{1,0:T(8,128)S(1)} collective-permute-done((f32[32,2048]{1,0:T(8,128)S(1)}, f32[32,2048]{1,0:T(8,128)S(1)}, u32[]{:S(2)}, u32[]{:S(2)}) %collective-permute-start.6) | collective-permute-done | bytes 262176 | tf_op jit(solution)/shard_map/ppermute | solution.py:45
  47.9 2.3 %collective-permute-start.12 = (f32[128,2048]{1,0:T(8,128)S(1)}, f32[128,2048]{1,0:T(8,128)S(1)}, u32[]{:S(2)}, u32[]{:S(2)}) collective-permute-start(f32[128,2048]{1,0:T(8,128)S(1)} %get-tuple-element.15), channel_id=1, source_target_pairs={{0,19},{32,44},{4,23},{36,32},{8,27},{40,36},{12,31},{44,40},{16,0... | collective-permute-start | bytes 3145736 | tf_op jit(solution)/shard_map/ppermute | solution.py:45
  50.5 2.6 %collective-permute-start.23 = (f32[4,8,8,512]{3,2,1,0:T(8,128)S(1)}, f32[4,8,8,512]{3,2,1,0:T(8,128)S(1)}, u32[]{:S(2)}, u32[]{:S(2)}) collective-permute-start(f32[4,8,8,512]{3,2,1,0:T(8,128)S(1)} %pad_maximum_fusion.own), channel_id=1, source_target_pairs={{0,64},{32,224},{64,128},{96,32},{128,192},{160,96},{192,0},{224,1... | collective-permute-start | bytes 1572872 | tf_op jit(solution)/shard_map/ppermute | solution.py:27
  53.1 6.1 %collective-permute-done.23.near = f32[4,8,8,512]{3,2,1,0:T(8,128)S(1)} collective-permute-done((f32[4,8,8,512]{3,2,1,0:T(8,128)S(1)}, f32[4,8,8,512]{3,2,1,0:T(8,128)S(1)}, u32[]{:S(2)}, u32[]{:S(2)}) %collective-permute-start.23) | collective-permute-done | bytes 524320 | tf_op jit(solution)/shard_map/ppermute | solution.py:27
  59.2 3.7 %collective-permute-start.25 = (f32[2,8,8,512]{3,2,1,0:T(8,128)S(1)}, f32[2,8,8,512]{3,2,1,0:T(8,128)S(1)}, u32[]{:S(2)}, u32[]{:S(2)}) collective-permute-start(f32[2,8,8,512]{3,2,1,0:T(8,128)S(1)} %slice_select_fusion.3), channel_id=1, source_target_pairs={{0,64},{32,224},{64,128},{96,32},{128,192},{160,96},{192,0},{224,1... | collective-permute-start | bytes 786440 | tf_op jit(solution)/shard_map/ppermute | solution.py:27
  62.9 1.0 fusion
  63.9 2.2 %collective-permute-start.16 = (f32[64,2048]{1,0:T(8,128)}, f32[64,2048]{1,0:T(8,128)}, u32[]{:S(2)}, u32[]{:S(2)}) collective-permute-start(f32[64,2048]{1,0:T(8,128)} %get-tuple-element.11), channel_id=1, source_target_pairs={{0,19},{32,44},{4,23},{36,32},{8,27},{40,36},{12,31},{44,40},{16,0... | collective-permute-start | bytes 1572872 | tf_op jit(solution)/shard_map/ppermute | solution.py:45
  66.1 2.2 %collective-permute-done.11.refs_12_ = f32[128,2048]{1,0:T(8,128)S(1)} collective-permute-done((f32[128,2048]{1,0:T(8,128)S(1)}, f32[128,2048]{1,0:T(8,128)S(1)}, u32[]{:S(2)}, u32[]{:S(2)}) %collective-permute-start.11) | collective-permute-done | bytes 1048608 | tf_op jit(solution)/shard_map/ppermute | solution.py:45
  68.3 1.2 %slice_select_fusion.1 = (f32[64,2048]{1,0:T(8,128)}, f32[64,2048]{1,0:T(8,128)}) fusion(f32[128,2048]{1,0:T(8,128)S(1)} %collective-permute-done.11.refs_12_, pred[]{:T(512)S(6)} %eq.392, f32[96,2048]{1,0:T(8,128)S(1)} %collective-permute-done.7.refs_8_), kind=kLoop, calls=%fused_computation.2 | loop fusion | flops 262144 | bytes 2621441 | tf_op jit(solution)/shard_map/jit(_where)/select_n | solution.py:191
  70.4 2.6 %collective-permute-start.15 = (f32[64,2048]{1,0:T(8,128)S(1)}, f32[64,2048]{1,0:T(8,128)}, u32[]{:S(2)}, u32[]{:S(2)}) collective-permute-start(f32[64,2048]{1,0:T(8,128)S(1)} %get-tuple-element.12), channel_id=1, source_target_pairs={{0,19},{32,44},{4,23},{36,32},{8,27},{40,36},{12,31},{44,40},{16,0... | collective-permute-start | bytes 1572872 | tf_op jit(solution)/shard_map/ppermute | solution.py:45
  73.0 1.5 %collective-permute-start.18 = (f32[64,2048]{1,0:T(8,128)}, f32[64,2048]{1,0:T(8,128)}, u32[]{:S(2)}, u32[]{:S(2)}) collective-permute-start(f32[64,2048]{1,0:T(8,128)} %collective-permute-done.16.refs_17_), channel_id=1, source_target_pairs={{0,19},{4,23},{8,27},{12,31},{16,0},{20,4},{24,8},{28,12},{1,16},{... | collective-permute-start | bytes 1572872 | tf_op jit(solution)/shard_map/ppermute | solution.py:45
  74.5 5.0 %collective-permute-done.13.refs_14_ = f32[64,2048]{1,0:T(8,128)} collective-permute-done((f32[64,2048]{1,0:T(8,128)}, f32[64,2048]{1,0:T(8,128)}, u32[]{:S(2)}, u32[]{:S(2)}) %collective-permute-start.13) | collective-permute-done | bytes 524320 | tf_op jit(solution)/shard_map/ppermute | solution.py:45
  79.5 1.5 %collective-permute-start.17 = (f32[64,2048]{1,0:T(8,128)}, f32[64,2048]{1,0:T(8,128)}, u32[]{:S(2)}, u32[]{:S(2)}) collective-permute-start(f32[64,2048]{1,0:T(8,128)} %collective-permute-done.13.refs_14_), channel_id=1, source_target_pairs={{0,16},{4,20},{8,24},{12,28},{16,1},{20,5},{24,9},{28,13},{1,17},{... | collective-permute-start | bytes 1572872 | tf_op jit(solution)/shard_map/ppermute | solution.py:45
  85.3 4.1 %shard_map.55 = (bf16[1024,512]{1,0:T(8,128)(2,1)}, bf16[1024,512]{1,0:T(8,128)(2,1)}) custom-call(s32[3]{0:T(128)} %pad_add_fusion.place, f32[4,8,8,512]{3,2,1,0:T(8,128)} %copy-done.1, f32[4,8,8,512]{3,2,1,0:T(8,128)} %copy-done.2, f32[4,8,8,512]{3,2,1,0:T(8,128)} %copy-done.6, f32[2,8,8,512]{3,2,1,0:T(8,128)} %copy-done.7, ...), custom_call_target="tpu_custom_call" | custom-call | tf_op jit(solution)/shard_map/pallas_call | solution.py:79
  89.5 14.4 %shard_map.56 = f32[2048,512]{1,0:T(8,128)} custom-call(s32[72]{0:T(128)} %stack.315.runs, f32[32,2048]{1,0:T(8,128)} %refs_0_.1, f32[32,2048]{1,0:T(8,128)} %copy-done.9, f32[32,2048]{1,0:T(8,128)} %copy-done.8, f32[32,2048]{1,0:T(8,128)} %copy-done.18, f32[32,2048]{1,0:T(8,128)} %copy-done.10, f32[32,2048]{1,0:T(8,128)} %copy-done.11, ...), custom_call_target="tpu_custom_call" | custom-call | flops 6442450944 | bytes 19922944 | tf_op jit(solution)/shard_map/pallas_call | solution.py:167
  (88 shorter events, 6.3 us)
Async XLA Ops:
  0.0 14.8 %collective-permute-start.1 = (f32[32,2048]{1,0:T(8,128)}, f32[32,2048]{1,0:T(8,128)S(1)}, u32[]{:S(2)}, u32[]{:S(2)}) collective-permute-start(f32[32,2048]{1,0:T(8,128)} %refs_0_.1), channel_id=1, source_target_pairs={{0,12},{32,51},{4,0},{36,55},{8,4},{40,59},{12,8},{44,63},{16,28},... | collective-permute-start | bytes 786440 | tf_op jit(solution)/shard_map/ppermute | solution.py:45
  6.4 10.3 %collective-permute-start = (f32[32,2048]{1,0:T(8,128)}, f32[32,2048]{1,0:T(8,128)S(1)}, u32[]{:S(2)}, u32[]{:S(2)}) collective-permute-start(f32[32,2048]{1,0:T(8,128)} %refs_0_.1), channel_id=1, source_target_pairs={{0,4},{32,48},{4,8},{36,52},{8,12},{40,56},{12,0},{44,60},{16,20},... | collective-permute-start | bytes 786440 | tf_op jit(solution)/shard_map/ppermute | solution.py:45
  7.4 11.0 %collective-permute-start.19 = (f32[8,4,512]{2,1,0:T(4,128)S(1)}, f32[8,4,512]{2,1,0:T(4,128)S(1)}, u32[]{:S(2)}, u32[]{:S(2)}) collective-permute-start(f32[8,4,512]{2,1,0:T(4,128)S(1)} %get-tuple-element.20), channel_id=1, source_target_pairs={{0,1},{1,2},{2,3},{3,0},{4,5},{5,6},{6,7},{7,4},{8,9},{9,10},{10,1... | collective-permute-start | bytes 196616 | tf_op jit(solution)/shard_map/ppermute | solution.py:210
  7.5 18.3 %collective-permute-start.21 = (f32[8,4,512]{2,1,0:T(4,128)S(1)}, f32[8,4,512]{2,1,0:T(4,128)S(1)}, u32[]{:S(2)}, u32[]{:S(2)}) collective-permute-start(f32[8,4,512]{2,1,0:T(4,128)S(1)} %get-tuple-element.21), channel_id=1, source_target_pairs={{0,3},{1,0},{2,1},{3,2},{4,7},{5,4},{6,5},{7,6},{8,11},{9,8},{10,9... | collective-permute-start | bytes 196616 | tf_op jit(solution)/shard_map/ppermute | solution.py:210
  11.0 14.7 %collective-permute-start.20 = (f32[8,4,512]{2,1,0:T(4,128)S(1)}, f32[8,4,512]{2,1,0:T(4,128)S(1)}, u32[]{:S(2)}, u32[]{:S(2)}) collective-permute-start(f32[8,4,512]{2,1,0:T(4,128)S(1)} %get-tuple-element.22), channel_id=1, source_target_pairs={{0,2},{1,3},{2,0},{3,1},{4,6},{5,7},{6,4},{7,5},{8,10},{9,11},{10,... | collective-permute-start | bytes 196616 | tf_op jit(solution)/shard_map/ppermute | solution.py:210
  14.8 33.0 %copy-start.8 = (f32[32,2048]{1,0:T(8,128)}, f32[32,2048]{1,0:T(8,128)S(1)}, u32[]{:S(2)}) copy-start(f32[32,2048]{1,0:T(8,128)S(1)} %collective-permute-done.1.refs_2_) | copy-start | bytes 786436
  14.8 12.5 %collective-permute-start.3 = (f32[32,2048]{1,0:T(8,128)S(1)}, f32[32,2048]{1,0:T(8,128)S(1)}, u32[]{:S(2)}, u32[]{:S(2)}) collective-permute-start(f32[32,2048]{1,0:T(8,128)S(1)} %collective-permute-done.1.refs_2_), channel_id=1, source_target_pairs={{32,51},{36,55},{40,59},{44,63},{48,32},{52,36},{56,40},{60,44},{3... | collective-permute-start | bytes 786440 | tf_op jit(solution)/shard_map/ppermute | solution.py:45
  16.8 6.8 %collective-permute-start.2 = (f32[32,2048]{1,0:T(8,128)S(1)}, f32[32,2048]{1,0:T(8,128)S(1)}, u32[]{:S(2)}, u32[]{:S(2)}) collective-permute-start(f32[32,2048]{1,0:T(8,128)S(1)} %collective-permute-done.refs_1_), channel_id=1, source_target_pairs={{0,4},{32,48},{4,8},{36,52},{8,12},{40,56},{12,0},{44,60},{16,20},... | collective-permute-start | bytes 786440 | tf_op jit(solution)/shard_map/ppermute | solution.py:45
  18.3 20.0 %collective-permute-start.9 = (f32[96,2048]{1,0:T(8,128)S(1)}, f32[96,2048]{1,0:T(8,128)S(1)}, u32[]{:S(2)}, u32[]{:S(2)}) collective-permute-start(f32[96,2048]{1,0:T(8,128)S(1)} %constant_dynamic-update-slice_fusion), channel_id=1, source_target_pairs={{0,19},{32,44},{4,23},{36,32},{8,27},{40,36},{12,31},{44,40},{16,0... | collective-permute-start | bytes 2359304 | tf_op jit(solution)/shard_map/ppermute | solution.py:45
  23.6 9.1 %collective-permute-start.4 = (f32[32,2048]{1,0:T(8,128)S(1)}, f32[32,2048]{1,0:T(8,128)S(1)}, u32[]{:S(2)}, u32[]{:S(2)}) collective-permute-start(f32[32,2048]{1,0:T(8,128)S(1)} %collective-permute-done.2.refs_3_), channel_id=1, source_target_pairs={{32,48},{36,52},{40,56},{44,60},{48,33},{52,37},{56,41},{60,45},{3... | collective-permute-start | bytes 786440 | tf_op jit(solution)/shard_map/ppermute | solution.py:45
  25.8 24.4 %collective-permute-start.22 = (f32[4,8,4,512]{3,2,1,0:T(4,128)S(1)}, f32[4,8,4,512]{3,2,1,0:T(4,128)S(1)}, u32[]{:S(2)}, u32[]{:S(2)}) collective-permute-start(f32[4,8,4,512]{3,2,1,0:T(4,128)S(1)} %pad_maximum_fusion.1), channel_id=1, source_target_pairs={{0,32},{32,0},{1,33},{33,1},{2,34},{34,2},{3,35},{35,3},{4,36},{36... | collective-permute-start | bytes 786440 | tf_op jit(solution)/shard_map/ppermute | solution.py:31
  27.1 20.5 %collective-permute-start.7 = (f32[96,2048]{1,0:T(8,128)S(1)}, f32[96,2048]{1,0:T(8,128)S(1)}, u32[]{:S(2)}, u32[]{:S(2)}) collective-permute-start(f32[96,2048]{1,0:T(8,128)S(1)} %constant_dynamic-update-slice_fusion), channel_id=1, source_target_pairs={{0,16},{32,36},{4,20},{36,40},{8,24},{40,44},{12,28},{44,32},{16,1... | collective-permute-start | bytes 2359304 | tf_op jit(solution)/shard_map/ppermute | solution.py:45
  27.3 10.0 %collective-permute-start.5 = (f32[32,2048]{1,0:T(8,128)S(1)}, f32[32,2048]{1,0:T(8,128)S(1)}, u32[]{:S(2)}, u32[]{:S(2)}) collective-permute-start(f32[32,2048]{1,0:T(8,128)S(1)} %collective-permute-done.3.refs_4_), channel_id=1, source_target_pairs={{32,51},{36,55},{40,59},{44,63},{48,32},{52,36},{56,40},{60,44},{3... | collective-permute-start | bytes 786440 | tf_op jit(solution)/shard_map/ppermute | solution.py:45
  32.7 8.3 %collective-permute-start.10 = (f32[32,2048]{1,0:T(8,128)S(1)}, f32[32,2048]{1,0:T(8,128)S(1)}, u32[]{:S(2)}, u32[]{:S(2)}) collective-permute-start(f32[32,2048]{1,0:T(8,128)S(1)} %collective-permute-done.2.refs_3_), channel_id=1, source_target_pairs={{0,19},{32,44},{4,23},{36,32},{8,27},{40,36},{12,31},{44,40},{16,0... | collective-permute-start | bytes 786440 | tf_op jit(solution)/shard_map/ppermute | solution.py:45
  37.3 9.6 %collective-permute-start.8 = (f32[32,2048]{1,0:T(8,128)S(1)}, f32[32,2048]{1,0:T(8,128)S(1)}, u32[]{:S(2)}, u32[]{:S(2)}) collective-permute-start(f32[32,2048]{1,0:T(8,128)S(1)} %collective-permute-done.2.refs_3_), channel_id=1, source_target_pairs={{0,16},{32,36},{4,20},{36,40},{8,24},{40,44},{12,28},{44,32},{16,1... | collective-permute-start | bytes 786440 | tf_op jit(solution)/shard_map/ppermute | solution.py:45
  38.4 8.5 %collective-permute-start.6 = (f32[32,2048]{1,0:T(8,128)S(1)}, f32[32,2048]{1,0:T(8,128)S(1)}, u32[]{:S(2)}, u32[]{:S(2)}) collective-permute-start(f32[32,2048]{1,0:T(8,128)S(1)} %collective-permute-done.4.refs_5_), channel_id=1, source_target_pairs={{32,48},{36,52},{40,56},{44,60},{48,33},{52,37},{56,41},{60,45},{3... | collective-permute-start | bytes 786440 | tf_op jit(solution)/shard_map/ppermute | solution.py:45
  47.9 15.0 %collective-permute-start.12 = (f32[128,2048]{1,0:T(8,128)S(1)}, f32[128,2048]{1,0:T(8,128)S(1)}, u32[]{:S(2)}, u32[]{:S(2)}) collective-permute-start(f32[128,2048]{1,0:T(8,128)S(1)} %get-tuple-element.15), channel_id=1, source_target_pairs={{0,19},{32,44},{4,23},{36,32},{8,27},{40,36},{12,31},{44,40},{16,0... | collective-permute-start | bytes 3145736 | tf_op jit(solution)/shard_map/ppermute | solution.py:45
  50.4 31.3 %copy-start.17 = (s32[8,128]{1,0:T(8,128)S(1)}, s32[8,128]{1,0:T(8,128)}, u32[]{:S(2)}) copy-start(s32[8,128]{1,0:T(8,128)} %param.8) | copy-start | bytes 12292
  50.5 34.0 %copy-start.1 = (f32[4,8,8,512]{3,2,1,0:T(8,128)}, f32[4,8,8,512]{3,2,1,0:T(8,128)S(1)}, u32[]{:S(2)}) copy-start(f32[4,8,8,512]{3,2,1,0:T(8,128)S(1)} %pad_maximum_fusion.own) | copy-start | bytes 1572868
  50.5 8.7 %collective-permute-start.23 = (f32[4,8,8,512]{3,2,1,0:T(8,128)S(1)}, f32[4,8,8,512]{3,2,1,0:T(8,128)S(1)}, u32[]{:S(2)}, u32[]{:S(2)}) collective-permute-start(f32[4,8,8,512]{3,2,1,0:T(8,128)S(1)} %pad_maximum_fusion.own), channel_id=1, source_target_pairs={{0,64},{32,224},{64,128},{96,32},{128,192},{160,96},{192,0},{224,1... | collective-permute-start | bytes 1572872 | tf_op jit(solution)/shard_map/ppermute | solution.py:27
  53.1 15.3 %collective-permute-start.11 = (f32[128,2048]{1,0:T(8,128)S(1)}, f32[128,2048]{1,0:T(8,128)S(1)}, u32[]{:S(2)}, u32[]{:S(2)}) collective-permute-start(f32[128,2048]{1,0:T(8,128)S(1)} %get-tuple-element.16), channel_id=1, source_target_pairs={{0,16},{32,36},{4,20},{36,40},{8,24},{40,44},{12,28},{44,32},{16,1... | collective-permute-start | bytes 3145736 | tf_op jit(solution)/shard_map/ppermute | solution.py:45
  59.2 25.3 %copy-start.2 = (f32[4,8,8,512]{3,2,1,0:T(8,128)}, f32[4,8,8,512]{3,2,1,0:T(8,128)S(1)}, u32[]{:S(2)}) copy-start(f32[4,8,8,512]{3,2,1,0:T(8,128)S(1)} %collective-permute-done.23.near) | copy-start | bytes 1572868
  59.2 10.4 %collective-permute-start.25 = (f32[2,8,8,512]{3,2,1,0:T(8,128)S(1)}, f32[2,8,8,512]{3,2,1,0:T(8,128)S(1)}, u32[]{:S(2)}, u32[]{:S(2)}) collective-permute-start(f32[2,8,8,512]{3,2,1,0:T(8,128)S(1)} %slice_select_fusion.3), channel_id=1, source_target_pairs={{0,64},{32,224},{64,128},{96,32},{128,192},{160,96},{192,0},{224,1... | collective-permute-start | bytes 786440 | tf_op jit(solution)/shard_map/ppermute | solution.py:27
  62.9 26.5 %copy-start.3 = (f32[128,2048]{1,0:T(8,128)}, f32[128,2048]{1,0:T(8,128)S(1)}, u32[]{:S(2)}) copy-start(f32[128,2048]{1,0:T(8,128)S(1)} %collective-permute-done.12.refs_13_) | copy-start | bytes 3145732
  63.9 9.1 %collective-permute-start.16 = (f32[64,2048]{1,0:T(8,128)}, f32[64,2048]{1,0:T(8,128)}, u32[]{:S(2)}, u32[]{:S(2)}) collective-permute-start(f32[64,2048]{1,0:T(8,128)} %get-tuple-element.11), channel_id=1, source_target_pairs={{0,19},{32,44},{4,23},{36,32},{8,27},{40,36},{12,31},{44,40},{16,0... | collective-permute-start | bytes 1572872 | tf_op jit(solution)/shard_map/ppermute | solution.py:45
  69.7 9.9 %collective-permute-start.13 = (f32[64,2048]{1,0:T(8,128)}, f32[64,2048]{1,0:T(8,128)}, u32[]{:S(2)}, u32[]{:S(2)}) collective-permute-start(f32[64,2048]{1,0:T(8,128)} %get-tuple-element.14), channel_id=1, source_target_pairs={{0,16},{32,36},{4,20},{36,40},{8,24},{40,44},{12,28},{44,32},{16,1... | collective-permute-start | bytes 1572872 | tf_op jit(solution)/shard_map/ppermute | solution.py:45
  69.7 3.3 %collective-permute-start.26 = (f32[2,8,8,512]{3,2,1,0:T(8,128)S(1)}, f32[2,8,8,512]{3,2,1,0:T(8,128)}, u32[]{:S(2)}, u32[]{:S(2)}) collective-permute-start(f32[2,8,8,512]{3,2,1,0:T(8,128)S(1)} %collective-permute-done.25.far), channel_id=1, source_target_pairs={{0,32},{32,0},{1,33},{33,1},{2,34},{34,2},{3,35},{35,3},{4,36},{36... | collective-permute-start | bytes 786440 | tf_op jit(solution)/shard_map/ppermute | solution.py:31
  69.9 14.6 %collective-permute-start.24 = (f32[4,8,8,512]{3,2,1,0:T(8,128)S(1)}, f32[4,8,8,512]{3,2,1,0:T(8,128)S(1)}, u32[]{:S(2)}, u32[]{:S(2)}) collective-permute-start(f32[4,8,8,512]{3,2,1,0:T(8,128)S(1)} %collective-permute-done.23.near), channel_id=1, source_target_pairs={{0,32},{32,0},{1,33},{33,1},{2,34},{34,2},{3,35},{35,3},{4,36},{36... | collective-permute-start | bytes 1572872 | tf_op jit(solution)/shard_map/ppermute | solution.py:31
  70.4 19.0 %collective-permute-start.15 = (f32[64,2048]{1,0:T(8,128)S(1)}, f32[64,2048]{1,0:T(8,128)}, u32[]{:S(2)}, u32[]{:S(2)}) collective-permute-start(f32[64,2048]{1,0:T(8,128)S(1)} %get-tuple-element.12), channel_id=1, source_target_pairs={{0,19},{32,44},{4,23},{36,32},{8,27},{40,36},{12,31},{44,40},{16,0... | collective-permute-start | bytes 1572872 | tf_op jit(solution)/shard_map/ppermute | solution.py:45
  73.0 16.4 %collective-permute-start.14 = (f32[64,2048]{1,0:T(8,128)}, f32[64,2048]{1,0:T(8,128)}, u32[]{:S(2)}, u32[]{:S(2)}) collective-permute-start(f32[64,2048]{1,0:T(8,128)} %get-tuple-element.13), channel_id=1, source_target_pairs={{0,16},{32,36},{4,20},{36,40},{8,24},{40,44},{12,28},{44,32},{16,1... | collective-permute-start | bytes 1572872 | tf_op jit(solution)/shard_map/ppermute | solution.py:45
  73.0 16.4 %collective-permute-start.18 = (f32[64,2048]{1,0:T(8,128)}, f32[64,2048]{1,0:T(8,128)}, u32[]{:S(2)}, u32[]{:S(2)}) collective-permute-start(f32[64,2048]{1,0:T(8,128)} %collective-permute-done.16.refs_17_), channel_id=1, source_target_pairs={{0,19},{4,23},{8,27},{12,31},{16,0},{20,4},{24,8},{28,12},{1,16},{... | collective-permute-start | bytes 1572872 | tf_op jit(solution)/shard_map/ppermute | solution.py:45
  79.5 10.0 %collective-permute-start.17 = (f32[64,2048]{1,0:T(8,128)}, f32[64,2048]{1,0:T(8,128)}, u32[]{:S(2)}, u32[]{:S(2)}) collective-permute-start(f32[64,2048]{1,0:T(8,128)} %collective-permute-done.13.refs_14_), channel_id=1, source_target_pairs={{0,16},{4,20},{8,24},{12,28},{16,1},{20,5},{24,9},{28,13},{1,17},{... | collective-permute-start | bytes 1572872 | tf_op jit(solution)/shard_map/ppermute | solution.py:45
  (14 other events, 171.4 us)
